TPU v7x, 256 devices: a whole 4x4x8 slice. The times are simulated.
256 devices in a mesh: row: 32 (over y, z), col: 8 (over x, core).
Axes of the slice: x: 4, y: 4, z: 8, core: 2. Of those that a mesh axis runs over, the one named last changes fastest.
Arguments:
- features: float32 [16, 1024, 128], P(None, 'col'), may hold values from -6 to 6
- lengthscales: float32 [128], replicated, may hold values from 8 to 32
- noise_var: float32 [16, 1024], P(None, 'col'), may hold values from 0.5 to 2
- component: float32 [4, 4096, 16, 1024], P(None, 'row', None, 'col'), may hold values from 0 to 1, as said below
- step_index: int32 [1], replicated, may hold values from 0 to 126
Outputs:
- panel_factor: float32 [4, 4096, 128], P(None, 'row', 'col')
- trailing: float32 [4, 4096, 16, 1024], P(None, 'row', None, 'col')
Inputs may be any that keep to these rules, and one draw needn't show every extreme that they name: component is symmetric and positive semi-definite with entries in [0, 1], so that covar is symmetric positive definite.
All inputs are finite; a program needn't handle non-finite values.
Results may differ from a plain program's by a relative error of at most 0.0003.
Values sent between devices are 32-bit elements; how exact they have to be, the bound alone decides.
A program may use at most 64 MiB of HBM per device.

v0:
```python
import jax
import jax.numpy as jnp
from jax import lax
from jax.sharding import PartitionSpec as P


def spread(value, axis, source):
    kept = jnp.where(lax.axis_index(axis) == source, value, 0).astype(value.dtype)
    return lax.psum(kept, axis)


def solve_panel(factor, blocks):
    count = blocks.shape[0]
    width = factor.shape[0]
    right_side = jnp.transpose(blocks, (2, 0, 1)).reshape(width, count * width)
    solved = lax.linalg.triangular_solve(factor, right_side, left_side=True, lower=True)
    return jnp.transpose(solved.reshape(width, count, width), (1, 2, 0))


def body(features, lengthscales, noise_var, component, step_index):
    row_count = lax.axis_size("row")
    col_count = lax.axis_size("col")
    row_index = lax.axis_index("row")
    col_index = lax.axis_index("col")
    col_blocks, width, depth = features.shape
    row_blocks = component.shape[0]
    stride = row_count // col_count
    panel_index = step_index[0]
    chosen = jnp.arange(row_blocks, dtype=jnp.int32) * stride + row_index // col_count
    picked = jnp.take(features, chosen, axis=0)
    row_features = spread(picked, "col", row_index % col_count)
    col_points = features / lengthscales
    row_points = row_features / lengthscales
    col_squares = jnp.sum(col_points * col_points, axis=2)
    row_squares = jnp.sum(row_points * row_points, axis=2)
    products = jnp.einsum(
        "kad,mbd->kamb",
        row_points,
        col_points,
        precision=lax.Precision.HIGHEST,
        preferred_element_type=jnp.float32,
    )
    distance = row_squares[:, :, None, None] + col_squares[None, None, :, :] - 2.0 * products
    kernel = jnp.exp(-0.5 * distance)
    row_block_ids = jnp.arange(row_blocks, dtype=jnp.int32) * row_count + row_index
    col_block_ids = jnp.arange(col_blocks, dtype=jnp.int32) * col_count + col_index
    offsets = jnp.arange(width, dtype=jnp.int32)
    row_ids = row_block_ids[:, None] * width + offsets[None, :]
    col_ids = col_block_ids[:, None] * width + offsets[None, :]
    same = row_ids[:, :, None, None] == col_ids[None, None, :, :]
    matrix_tiles = kernel + component + jnp.where(same, noise_var[None, None, :, :], 0.0)
    col_slot = panel_index // col_count
    row_slot = panel_index // row_count
    column_tiles = lax.dynamic_index_in_dim(matrix_tiles, col_slot, axis=2, keepdims=False)
    diagonal = lax.dynamic_index_in_dim(column_tiles, row_slot, axis=0, keepdims=False)
    local_factor = jnp.linalg.cholesky(diagonal)
    row_factor = spread(local_factor, "col", panel_index % col_count)
    column_factor = spread(local_factor, "row", panel_index % row_count)
    local_panel = solve_panel(column_factor, column_tiles)
    row_panel = spread(local_panel, "col", panel_index % col_count)
    gathered = lax.all_gather(row_panel, "row", axis=1, tiled=True)
    grouped = gathered.reshape(row_blocks, stride, col_count, width, width)
    column_panel = lax.dynamic_index_in_dim(grouped, col_index, axis=2, keepdims=False).reshape(
        col_blocks, width, width
    )
    before = (row_block_ids < panel_index)[:, None, None]
    at_panel = (row_block_ids == panel_index)[:, None, None]
    panel_whole = jnp.where(before, 0.0, jnp.where(at_panel, row_factor[None, :, :], row_panel))
    share = width // col_count
    panel_factor = lax.dynamic_slice_in_dim(panel_whole, col_index * share, share, 2)
    masked_rows = jnp.where((row_block_ids > panel_index)[:, None, None], row_panel, 0.0)
    masked_cols = jnp.where((col_block_ids > panel_index)[:, None, None], column_panel, 0.0)
    update = jnp.einsum(
        "kab,mcb->kamc",
        masked_rows,
        masked_cols,
        precision=lax.Precision.HIGHEST,
        preferred_element_type=jnp.float32,
    )
    trailing = matrix_tiles - update
    return (panel_factor, trailing)


def solution(mesh):
    in_specs = (P(None, "col", None), P(), P(None, "col"), P(None, "row", None, "col"), P())
    out_specs = (P(None, "row", "col"), P(None, "row", None, "col"))
    return jax.shard_map(body, mesh=mesh, in_specs=in_specs, out_specs=out_specs, check_vma=False)
```

profile of v0, /device:TPU:1, one launch (start us, length us, event | category | flops | bytes accessed | tf_op | source)
XLA Modules:
  0.0 437.4 jit_solution(8704167523128326238)
XLA Ops:
  7.2 0.0 all-reduce.5.cloned.1.call-start
  7.3 1.8 gather_fusion
  9.1 0.8 select_select_fusion
  9.9 0.0 all-reduce.5.cloned.1.call-update
  9.9 0.0 all-reduce.7.cloned.1.call-start
  10.7 0.1 iota_add_fusion
  10.7 1.6 multiply_reduce_fusion
  12.4 0.1 iota_add_fusion.1
  12.5 65.1 %all-reduce.5.cloned.1.call-done = f32[4,128,128]{2,1,0:T(8,128)} async-done(((f32[4,128,128]{2,1,0:T(8,128)}), f32[4,128,128]{2,1,0:T(8,128)}) %all-reduce.5.cloned.1.call-update) | async-done | bytes 262160 | tf_op jit(solution)/shard_map/psum | solution.py:9
  77.5 1.1 multiply_reduce_fusion.1
  78.6 8.1 %fusion = f32[4,128,16,128]{3,1,2,0:T(8,128)S(1)} fusion(f32[4,128,16,128]{3,2,1,0:T(8,128)} %param.8, f32[16,128]{1,0:T(8,128)} %param.7, s32[16,128]{1,0:T(8,128)S(1)} %iota_add_fusion, s32[4,128]{1,0:T(4,128)S(1)} %iota_add_fusion.1, f32[16,128]{1,0:T(8,128)S(1)} %multiply_reduce_fusion, f32[4,128]{1,0:T(4,128)S(1)} %multiply_reduce_fusion.1, ...), kind=kOutput, calls=%fused_computation.2 | convolution fusion | flops 1619329024 | bytes 9728512 | tf_op jit(solution)/shard_map/kad,mbd->kamb/dot_general | solution.py:36
  86.7 0.0 copy-start
  86.7 2.0 copy-done
  88.7 0.1 copy.8
  88.8 0.9 fusion.12
  89.7 11.7 %cholesky.18 = f32[128,128]{1,0:T(8,128)S(1)} custom-call(f32[128,128]{1,0:T(8,128)S(1)} %fusion.12), custom_call_target="Cholesky" | custom-call | tf_op jit(solution)/shard_map/jit(cholesky)/cholesky | solution.py:56
  101.4 0.7 compare_reduce_fusion
  102.1 1.3 fusion.14
  103.4 0.0 all-reduce.7.cloned.1.call-update
  103.4 0.2 all-reduce.9.cloned.1.call-start
  103.6 136.1 %all-reduce.7.cloned.1.call-done = f32[128,128]{1,0:T(8,128)} async-done(((f32[128,128]{1,0:T(8,128)}), f32[128,128]{1,0:T(8,128)}) %all-reduce.7.cloned.1.call-update) | async-done | bytes 65552 | tf_op jit(solution)/shard_map/psum | solution.py:9
  239.8 0.8 select_bitcast_fusion
  240.6 9.8 %custom-call.6 = f32[1,128,128]{1,2,0:T(8,128)S(1)} custom-call(f32[1,128,128]{2,1,0:T(8,128)S(1)} %select_bitcast_fusion), custom_call_target="InvertDiagBlocksLowerTriangular" | custom-call | tf_op jit(solution)/shard_map/triangular_solve | solution.py:16
  250.4 2.0 convolution_select_fusion
  252.5 0.0 all-reduce.9.cloned.1.call-update
  252.5 0.0 all-gather.2.cloned.1.call-start
  252.5 65.7 %all-reduce.9.cloned.1.call-done = (f32[4,128,128]{2,1,0:T(8,128)}, f32[128,128]{1,0:T(8,128)}) async-done(((f32[4,128,128]{2,1,0:T(8,128)}, f32[128,128]{1,0:T(8,128)}), (f32[4,128,128]{2,1,0:T(8,128)}, f32[128,128]{1,0:T(8,128)})) %all-reduce.9.cloned.1.call-update) | async-done | bytes 327696 | tf_op jit(solution)/shard_map/psum | solution.py:9
  318.2 0.0 copy-start.2
  318.2 0.0 all-gather.2.cloned.1.call-update
  318.3 1.0 constant_dynamic-slice_fusion
  319.2 1.1 fusion.3
  320.4 0.7 copy.11
  321.1 99.0 %all-gather.2.cloned.1.call-done = f32[4,4096,128]{2,1,0:T(8,128)} async-done(((f32[4,128,128]{2,1,0:T(8,128)}), f32[4,4096,128]{2,1,0:T(8,128)}) %all-gather.2.cloned.1.call-update) | async-done | bytes 8388624 | tf_op jit(solution)/shard_map/all_gather | solution.py:61
  420.1 0.0 copy-start.1
  420.1 1.5 constant_dynamic-slice_fusion.1
  421.6 0.1 bitcast_select_fusion
  421.7 0.0 copy-done.2
  421.7 0.9 copy-done.1
  422.6 3.8 convolution_subtract_fusion
  426.4 4.4 %copy.12 = f32[4,128,16,128]{3,2,1,0:T(8,128)} copy(f32[4,128,16,128]{3,1,2,0:T(8,128)S(1)} %convolution_subtract_fusion) | data formatting | bytes 8388608
  (10 shorter events, 0.1 us)
Async XLA Ops:
  7.2 70.4 %all-reduce.5.cloned.1.call-start = ((), (), s32[]{:S(2)}) async-start(), calls=%async_computation | async-start | bytes 524288 | tf_op jit(solution)/shard_map/psum | solution.py:9
  9.9 229.9 %all-reduce.7.cloned.1.call-start = ((), (), s32[]{:S(2)}) async-start(), calls=%async_computation.1 | async-start | bytes 131072 | tf_op jit(solution)/shard_map/psum | solution.py:9
  86.7 2.0 copy-start
  103.4 214.8 %all-reduce.9.cloned.1.call-start = ((), (), s32[]{:S(2)}) async-start(), calls=%async_computation.3 | async-start | bytes 655360 | tf_op jit(solution)/shard_map/psum | solution.py:9
  252.5 167.6 %all-gather.2.cloned.1.call-start = ((), (), s32[]{:S(2)}) async-start(), calls=%async_computation.2 | async-start | bytes 8650752 | tf_op jit(solution)/shard_map/all_gather | solution.py:61
  318.2 103.5 %copy-start.2 = (f32[4,128,128]{2,1,0:T(8,128)S(1)}, f32[4,128,128]{2,1,0:T(8,128)}, u32[]{:S(2)}) copy-start(f32[4,128,128]{2,1,0:T(8,128)} %get-tuple-element.4) | copy-start | bytes 786436
  420.1 2.5 copy-start.1
Sparse Core Ops, SparseCore 0:
  10.9 66.5 all-reduce.4
  103.5 136.2 all-reduce.6
  252.6 65.5 all-reduce.8
  320.7 99.3 all-gather.1
where the time goes:
time: 438 us; the launch traced here: 437 us
  waiting for transfers between devices  366 us (84%)
  other arithmetic  30.1 us (7%)
  between operations  14.7 us (3%)
  matrix products  13.9 us (3%)
  local copies, waits for them, and re-layouts  12.4 us (3%)
    psum x3, waiting for transfers between devices, spread(): return lax.psum(kept, axis)  267 us
    all_gather x1, waiting for transfers between devices, body(): gathered = lax.all_gather(row_panel, 'row', axis=1, tiled=True)  99 us
    another operation x3, other arithmetic, body(): local_factor = jnp.linalg.cholesky(diagonal)  12.4 us
    another operation x2, other arithmetic, solve_panel(): lax.linalg.triangular_solve(factor, right_side, left_side=True, lower=True)  10.7 us
  transfers between devices with their start and end apart: 4, of which 4 were waited for; matrix products, arithmetic and copies ran while one was open for 1% of the time, Pallas kernels for 0%

commit v1 on v0

v1 whole, which is shorter than its diff:
```python
import functools

import jax
import jax.numpy as jnp
from jax import lax
from jax.experimental import pallas as pl
from jax.experimental.pallas import tpu as pltpu
from jax.sharding import PartitionSpec as P

MESH = pl.DeviceIdType.MESH
F32 = jnp.float32
BF16 = jnp.bfloat16
B = 128
KR, KC, NR, NC = 4, 16, 32, 8
NY, NZ = 4, 8
PART = B // NC
PANEL = KR * PART
XROWS = PANEL + PART + 8
VMEM_LIMIT = 56 * 1024 * 1024


def split3(x):
    high = x.astype(BF16)
    rest = x - high.astype(F32)
    mid = rest.astype(BF16)
    low = (rest - mid.astype(F32)).astype(BF16)
    return high, mid, low


def left6(x, axis=1):
    h, m, l = split3(x)
    return jnp.concatenate([h, h, m, h, m, l], axis=axis)


def right6(x, axis=1):
    h, m, l = split3(x)
    return jnp.concatenate([h, m, h, l, m, h], axis=axis)


def dot_nt(a, b):
    return lax.dot_general(a, b, (((1,), (1,)), ((), ())), preferred_element_type=F32)


def lane_squares(points):
    cat = jnp.concatenate(split3(points * points), axis=1)
    ones = jnp.ones((16, cat.shape[1]), BF16)
    return dot_nt(ones, cat)[0:8, :]


def factor_inverse(w_ref, dv_ref):
    size = 16
    lane = lax.broadcasted_iota(jnp.int32, (size, B), 1)
    row = lax.broadcasted_iota(jnp.int32, (size, B), 0)

    def block(b, carry):
        start = pl.multiple_of(b * size, size)
        rows = pl.ds(start, size)
        left = w_ref[rows, 0:B]
        right = w_ref[rows, B : 2 * B]
        rolled = pltpu.roll(left, lax.rem(B - start, B), axis=1)
        cols = [jnp.broadcast_to(rolled[:, k : k + 1], (size, B)) for k in range(size)]
        inv = jnp.zeros((size, B), F32)
        for k in range(size):
            pivot = jnp.broadcast_to(cols[k][k : k + 1, :], (size, B))
            rinv = 1.0 / pivot
            inv = jnp.where(row == k, rinv, inv)
            mult = jnp.where(row > k, cols[k] * rinv, 0.0)
            for j in range(k + 1, size):
                cols[j] = cols[j] - mult * cols[j][k : k + 1, :]
            left = left - mult * left[k : k + 1, :]
            right = right - mult * right[k : k + 1, :]
        w_ref[rows, 0:B] = left
        w_ref[rows, B : 2 * B] = right
        dv_ref[rows, :] = inv
        scaled = jnp.where(lane >= start + size, left * inv, 0.0)
        update = lax.dot_general(
            left6(scaled, 0),
            right6(jnp.concatenate([left, right], axis=1), 0),
            (((0,), (0,)), ((), ())),
            preferred_element_type=F32,
        )
        w_ref[...] = w_ref[...] - update
        return carry

    lax.fori_loop(0, B // size, block, 0)
    return w_ref[:, B : 2 * B] * jnp.sqrt(dv_ref[...])


def gather_kernel(
    step_ref,
    feat_ref,
    ls_ref,
    noise_ref,
    comp_ref,
    covar_ref,
    linv_ref,
    rowc_ref,
    colc_ref,
    comp_v,
    feat_v,
    s_a,
    r_a,
    z_a,
    y_a,
    diag,
    s_b,
    r_b,
    g_b,
    colall,
    rowfeat,
    colcat,
    rowcat,
    sqcol,
    covar_v,
    w_v,
    dv_v,
    local_sem,
    send_sem,
    recv_sem,
):
    r = lax.axis_index("row")
    c = lax.axis_index("col")
    z = lax.rem(r, NZ)
    y = lax.div(r, NZ)

    def at_x(i):
        return (r, i)

    def at_z(i):
        return (y * NZ + i, c)

    def at_y(i):
        return (i * NZ + z, c)

    partner = (y * NZ + c, z)

    def other(me, d, n):
        return lax.rem(me + d, n)

    feat_copy = pltpu.make_async_copy(feat_ref, feat_v, local_sem.at[0])
    comp_copy = pltpu.make_async_copy(comp_ref, comp_v, local_sem.at[1])
    comp_copy.start()
    feat_copy.start()

    barrier = pltpu.get_barrier_semaphore()
    for d in range(1, NC):
        pl.semaphore_signal(barrier, inc=1, device_id=at_x(other(c, d, NC)), device_id_type=MESH)
    for d in range(1, NZ):
        pl.semaphore_signal(barrier, inc=1, device_id=at_z(other(z, d, NZ)), device_id_type=MESH)
    for d in range(1, NY):
        pl.semaphore_signal(barrier, inc=1, device_id=at_y(other(y, d, NY)), device_id_type=MESH)

    @pl.when(z != c)
    def _():
        pl.semaphore_signal(barrier, inc=1, device_id=partner, device_id_type=MESH)

    def remote(src, dst, slot, recv, dev):
        return pltpu.make_async_remote_copy(
            src_ref=src,
            dst_ref=dst,
            send_sem=send_sem.at[slot],
            recv_sem=recv_sem.at[recv],
            device_id=dev,
            device_id_type=MESH,
        )

    waits = []

    def spread(src, dst, off, n, me, dev):
        for d in range(1, n):
            peer = other(me, d, n)
            copy = remote(src(peer), dst(me), off + d, off + me, dev(peer))
            copy.start()
            waits.append(copy)

    def arrived(dst, off, n, me, dev):
        for d in range(1, n):
            peer = other(me, d, n)
            remote(dst(peer), dst(peer), off + d, off + peer, dev(peer)).wait_recv()

    p = step_ref[0]
    panel_m = lax.div(p, NC)
    panel_c = lax.rem(p, NC)
    panel_k = lax.div(p, NR)
    panel_r = lax.rem(p, NR)
    panel_z = lax.rem(panel_r, NZ)
    panel_y = lax.div(panel_r, NZ)
    inv_ls = 1.0 / ls_ref[...]

    comp_copy.wait()
    cand = comp_v[pl.ds(panel_k * (B * KC) + panel_m, B, stride=KC), :]
    s_a[...] = cand.reshape(NC, PART, B)
    for k in range(KR):
        block = comp_v[pl.ds(k * (B * KC) + panel_m, B, stride=KC), :]
        s_b[:, k * PART : (k + 1) * PART, :] = block.reshape(NC, PART, B)
    feat_copy.wait()
    feat_p = feat_v[lax.div(panel_m, 4), lax.rem(panel_m, 4)] * inv_ls
    s_b[:, PANEL : PANEL + PART, :] = feat_p.reshape(NC, PART, B)
    noise_p = noise_ref[pl.ds(panel_m, 1), :]
    s_b[:, PANEL + PART : XROWS, :] = jnp.broadcast_to(noise_p.reshape(1, 1, B), (NC, 8, B))
    r_a[c] = s_a[c]
    r_b[c] = s_b[c]

    @pl.when(z != c)
    def _():
        pl.semaphore_wait(barrier, 2 * NC + NY - 2)

    @pl.when(z == c)
    def _():
        pl.semaphore_wait(barrier, 2 * NC + NY - 3)

    spread(lambda i: s_a.at[i], lambda i: r_a.at[i], 0, NC, c, at_x)
    spread(lambda i: s_b.at[i], lambda i: r_b.at[i], 8, NC, c, at_x)

    feat_move = [remote(feat_v.at[k, y], rowfeat.at[k], 80 + k, 80 + k, partner) for k in range(KR)]

    @pl.when(z != c)
    def _():
        for copy in feat_move:
            copy.start()

    @pl.when(z == c)
    def _():
        for k in range(KR):
            rowfeat[k] = feat_v[k, y]

    def prepare(m, carry):
        pts = feat_v[lax.div(m, 4), lax.rem(m, 4)] * inv_ls
        colcat[pl.ds(pl.multiple_of(m * B, B), B), :] = right6(pts)
        sqcol[m] = lane_squares(pts)
        return carry

    arrived(lambda i: r_a.at[i], 0, NC, c, at_x)
    z_a[z] = r_a[panel_c]
    spread(lambda i: z_a.at[z], lambda i: z_a.at[i], 16, NZ, z, at_z)
    lax.fori_loop(0, KC // 2, prepare, 0)

    arrived(lambda i: r_b.at[i], 8, NC, c, at_x)
    g_b[c] = r_b[panel_c]
    move = remote(g_b.at[c, 0:PANEL], colall.at[y, c], 24, 24, partner)
    moved = remote(g_b.at[c, 0:PANEL], colall.at[y, z], 24, 24, partner)

    @pl.when(z != c)
    def _():
        move.start()

    @pl.when(z == c)
    def _():
        colall[y, z] = g_b[c, 0:PANEL, :]

    spread(lambda i: g_b.at[c], lambda i: g_b.at[i], 32, NC, c, at_x)

    arrived(lambda i: z_a.at[i], 16, NZ, z, at_z)
    y_a[y] = z_a[panel_z]
    spread(lambda i: y_a.at[y], lambda i: y_a.at[i], 40, NY, y, at_y)

    @pl.when(z != c)
    def _():
        moved.wait_recv()

    spread(lambda i: colall.at[y, z], lambda i: colall.at[y, i], 48, NZ, z, at_z)
    lax.fori_loop(KC // 2, KC, prepare, 0)

    arrived(lambda i: y_a.at[i], 40, NY, y, at_y)
    diag[c] = y_a[panel_y]
    spread(lambda i: diag.at[c], lambda i: diag.at[i], 56, NC, c, at_x)

    arrived(lambda i: colall.at[y, i], 48, NZ, z, at_z)
    spread(lambda i: colall.at[y], lambda i: colall.at[i], 64, NY, y, at_y)

    @pl.when(z != c)
    def _():
        for copy in feat_move:
            copy.wait_recv()

    half_row = []
    for k in range(KR):
        pts = rowfeat[k] * inv_ls
        rowcat[k * B : (k + 1) * B, :] = left6(pts)
        half_row.append(0.5 * jnp.sum(pts * pts, axis=1, keepdims=True))
    eye = lax.broadcasted_iota(jnp.int32, (B, B), 0) == lax.broadcasted_iota(jnp.int32, (B, B), 1)

    def cover(m2, carry):
        cols = colcat[pl.ds(pl.multiple_of(m2 * 2 * B, 2 * B), 2 * B), :]
        for k in range(KR):
            prod = dot_nt(rowcat[k * B : (k + 1) * B, :], cols)
            for j in range(2):
                m = m2 * 2 + j
                half_col = 0.5 * sqcol[m][0:1, :]
                expo = prod[:, j * B : (j + 1) * B] - (half_row[k] + half_col)
                value = jnp.exp(expo) + comp_v[pl.ds(k * (B * KC) + m, B, stride=KC), :]
                same = jnp.logical_and(z == c, m == k * 4 + y)
                added = jnp.where(jnp.logical_and(eye, same), noise_ref[pl.ds(m, 1), :], 0.0)
                covar_v[k * KC + m] = value + added
        return carry

    lax.fori_loop(0, KC // 2, cover, 0)
    covar_copy = pltpu.make_async_copy(covar_v, covar_ref, local_sem.at[2])
    covar_copy.start()

    arrived(lambda i: g_b.at[i], 32, NC, c, at_x)
    pts_p = g_b[:, PANEL : PANEL + PART, :].reshape(B, B)
    noise_full = g_b[0, PANEL + PART : PANEL + PART + 1, :]
    left_p, right_p = left6(pts_p), right6(pts_p)
    half_p = 0.5 * lane_squares(pts_p)[0:1, :]
    half_p_col = 0.5 * jnp.sum(pts_p * pts_p, axis=1, keepdims=True)
    kernel_p = jnp.exp(dot_nt(left_p, right_p) - (half_p_col + half_p))
    noise_p = jnp.where(eye, noise_full, 0.0)
    arrived(lambda i: diag.at[i], 56, NC, c, at_x)
    w_v[:, 0:B] = kernel_p + diag[...].reshape(B, B) + noise_p
    w_v[:, B : 2 * B] = jnp.where(eye, 1.0, 0.0)
    linv_ref[...] = factor_inverse(w_v, dv_v)

    for k in range(KR):
        kern = jnp.exp(dot_nt(rowcat[k * B : (k + 1) * B, :], right_p) - (half_row[k] + half_p))
        raw = g_b[:, k * PART : (k + 1) * PART, :].reshape(B, B)
        here = k * NR + r == p
        rowc_ref[k] = kern + raw + jnp.where(here, noise_p, 0.0)

    def column(m, carry):
        pts = feat_v[lax.div(m, 4), lax.rem(m, 4)] * inv_ls
        half = 0.5 * jnp.sum(pts * pts, axis=1, keepdims=True)
        cols = colcat[pl.ds(pl.multiple_of(m * B, B), B), :]
        colc_ref[m] = jnp.exp(dot_nt(cols, left_p) - (half + half_p))
        return carry

    lax.fori_loop(0, KC, column, 0)
    arrived(lambda i: colall.at[i], 64, NY, y, at_y)
    for m in range(KC):
        k, q = m // NY, m % NY
        colc_ref[m] = colc_ref[m] + colall[q, :, k * PART : (k + 1) * PART, :].reshape(B, B)

    covar_copy.wait()
    for copy in waits:
        copy.wait_send()

    @pl.when(z != c)
    def _():
        move.wait_send()
        for copy in feat_move:
            copy.wait_send()


def update_kernel(step_ref, linv_ref, rowc_ref, colc_ref, covar_ref, pf_ref, out_ref, srow, scol):
    r = lax.axis_index("row")
    c = lax.axis_index("col")
    p = step_ref[0]
    step = pl.program_id(0)

    @pl.when(step == 0)
    def _():
        inverse = right6(linv_ref[...])
        share = right6(linv_ref[pl.ds(pl.multiple_of(c * PART, PART), PART), :])
        row = lax.broadcasted_iota(jnp.int32, (PART, B), 1)
        col = lax.broadcasted_iota(jnp.int32, (PART, B), 0) + c * PART
        for k in range(KR):
            w = k * NR + r
            left = left6(rowc_ref[k])
            solved = jnp.where(w > p, dot_nt(left, inverse), 0.0)
            h, m, _ = split3(solved)
            srow[k * B : (k + 1) * B, :] = jnp.concatenate([h, h, m], axis=1)
            mine = dot_nt(share, left)
            keep = jnp.logical_or(w > p, jnp.logical_and(w == p, col <= row))
            pf_ref[k] = jnp.where(keep, mine, 0.0)

        def column(i, carry):
            u = i * NC + c
            solved = jnp.where(u > p, dot_nt(left6(colc_ref[i]), inverse), 0.0)
            h, m, _ = split3(solved)
            scol[pl.ds(pl.multiple_of(i * B, B), B), :] = jnp.concatenate([h, m, h], axis=1)
            return carry

        lax.fori_loop(0, KC, column, 0)

    rows = srow[pl.ds(pl.multiple_of(step * B, B), B), :]

    def pair(m2, carry):
        cols = scol[pl.ds(pl.multiple_of(m2 * 2 * B, 2 * B), 2 * B), :]
        update = dot_nt(rows, cols)
        for j in range(2):
            m = m2 * 2 + j
            out_ref[pl.ds(m, B, stride=KC), :] = covar_ref[m] - update[:, j * B : (j + 1) * B]
        return carry

    lax.fori_loop(0, KC // 2, pair, 0)


def body(features, lengthscales, noise_var, component, step_index):
    any_spec = pl.BlockSpec(memory_space=pl.ANY)
    vmem = pl.BlockSpec(memory_space=pltpu.VMEM)
    smem = pl.BlockSpec(memory_space=pltpu.SMEM)
    covar, linv, rowc, colc = pl.pallas_call(
        gather_kernel,
        out_shape=(
            jax.ShapeDtypeStruct((KR * KC, B, B), F32),
            jax.ShapeDtypeStruct((B, B), F32),
            jax.ShapeDtypeStruct((KR, B, B), F32),
            jax.ShapeDtypeStruct((KC, B, B), F32),
        ),
        in_specs=[smem, any_spec, vmem, vmem, any_spec],
        out_specs=(any_spec, vmem, vmem, vmem),
        scratch_shapes=[
            pltpu.VMEM((KR * B * KC, B), F32),
            pltpu.VMEM((4, 4, B, B), F32),
            pltpu.VMEM((NC, PART, B), F32),
            pltpu.VMEM((NC, PART, B), F32),
            pltpu.VMEM((NZ, PART, B), F32),
            pltpu.VMEM((NY, PART, B), F32),
            pltpu.VMEM((NC, PART, B), F32),
            pltpu.VMEM((NC, XROWS, B), F32),
            pltpu.VMEM((NC, XROWS, B), F32),
            pltpu.VMEM((NC, XROWS, B), F32),
            pltpu.VMEM((NY, NZ, PANEL, B), F32),
            pltpu.VMEM((KR, B, B), F32),
            pltpu.VMEM((KC * B, 6 * B), BF16),
            pltpu.VMEM((KR * B, 6 * B), BF16),
            pltpu.VMEM((KC, 8, B), F32),
            pltpu.VMEM((KR * KC, B, B), F32),
            pltpu.VMEM((B, 2 * B), F32),
            pltpu.VMEM((B, B), F32),
            pltpu.SemaphoreType.DMA((3,)),
            pltpu.SemaphoreType.DMA((88,)),
            pltpu.SemaphoreType.DMA((88,)),
        ],
        compiler_params=pltpu.CompilerParams(
            collective_id=0, has_side_effects=True, vmem_limit_bytes=VMEM_LIMIT
        ),
        name="gather_panel",
    )(
        step_index,
        features.reshape(4, 4, B, B),
        lengthscales.reshape(1, B),
        noise_var,
        component.reshape(KR * B * KC, B),
    )
    pf, trailing = pl.pallas_call(
        update_kernel,
        grid=(KR,),
        out_shape=(
            jax.ShapeDtypeStruct((KR, PART, B), F32),
            jax.ShapeDtypeStruct((KR * B * KC, B), F32),
        ),
        in_specs=[
            smem,
            vmem,
            vmem,
            vmem,
            pl.BlockSpec((KC, B, B), lambda k: (k, 0, 0)),
        ],
        out_specs=(
            vmem,
            pl.BlockSpec((B * KC, B), lambda k: (k, 0)),
        ),
        scratch_shapes=[
            pltpu.VMEM((KR * B, 3 * B), BF16),
            pltpu.VMEM((KC * B, 3 * B), BF16),
        ],
        compiler_params=pltpu.CompilerParams(vmem_limit_bytes=VMEM_LIMIT),
        name="update_blocks",
    )(step_index, linv, rowc, colc, covar)
    return jnp.swapaxes(pf, 1, 2), trailing.reshape(KR, B, KC, B)


def solution(mesh):
    in_specs = (P(None, "col", None), P(), P(None, "col"), P(None, "row", None, "col"), P())
    out_specs = (P(None, "row", "col"), P(None, "row", None, "col"))
    return jax.shard_map(body, mesh=mesh, in_specs=in_specs, out_specs=out_specs, check_vma=False)
```

time: 438 us -> 74.4 us (0.17)
  the two profiles are of different devices: /device:TPU:1 before, /device:TPU:3 now
where the time goes in v1:
time: 74.4 us; the launch traced here: 74.2 us
  Pallas kernels  73 us (98%)
  between operations  1.29 us (2%)
    pallas_call x1, Pallas kernels, body(): pl.pallas_call(gather_kernel, out_shape=(jax.ShapeDtypeStruct((KR * KC, B...  58.5 us
    pallas_call x1, Pallas kernels, body(): pl.pallas_call(update_kernel, grid=(KR,), out_shape=(jax.ShapeDtypeStruct...  14.4 us

profile of v1, /device:TPU:3, one launch (start us, length us, event | category | flops | bytes accessed | tf_op | source)
XLA Modules:
  0.0 74.2 jit_solution(1184475077068920673)
XLA Ops:
  1.3 58.5 %gather_panel.1 = (f32[64,128,128]{2,1,0:T(8,128)}, f32[128,128]{1,0:T(8,128)}, f32[4,128,128]{2,1,0:T(8,128)}, f32[16,128,128]{2,1,0:T(8,128)}) custom-call(s32[1]{0:T(128)S(6)} %copy.7.step_ref, f32[4,4,128,128]{3,2,1,0:T(8,128)} %bitcast.6, f32[1,128]{1,0:T(1,128)} %bitcast.7, f32[16,128]{1,0:T(8,128)} %noise_ref.1, f32[8192,128]{1,0:T(8,128)} %bitcast.5), custom_call_target="tpu_custom_call" | custom-call | tf_op jit(solution)/shard_map/gather_panel/pallas_call | solution.py:392
  59.8 14.4 %update_blocks.1 = (f32[4,16,128]{2,1,0:T(8,128)}, f32[8192,128]{1,0:T(8,128)}) custom-call(s32[1]{0:T(128)S(6)} %copy.7.step_ref, f32[128,128]{1,0:T(8,128)} %get-tuple-element.8.linv_ref, f32[4,128,128]{2,1,0:T(8,128)} %get-tuple-element.9.rowc_ref, f32[16,128,128]{2,1,0:T(8,128)} %get-tuple-element.10.colc_ref, f32[64,128,128]{2,1,0:T(8,128)} %get-tuple-element.11.covar_ref), custom_call_target="tpu_custom_call" | custom-call | tf_op jit(solution)/shard_map/update_blocks/pallas_call | solution.py:436

commit v2 on v1

v2 whole, which is shorter than its diff:
```python
import functools

import jax
import jax.numpy as jnp
from jax import lax
from jax.experimental import pallas as pl
from jax.experimental.pallas import tpu as pltpu
from jax.sharding import PartitionSpec as P

MESH = pl.DeviceIdType.MESH
F32 = jnp.float32
BF16 = jnp.bfloat16
B = 128
KR, KC, NR, NC = 4, 16, 32, 8
NY, NZ = 4, 8
PART = B // NC
PANEL = KR * PART
FROWS = PART + 8
DEPTH = 5 * B
GATHER_VMEM = 40 * 1024 * 1024
UPDATE_VMEM = 16 * 1024 * 1024


def split2(x):
    high = x.astype(BF16)
    return high, (x - high.astype(F32)).astype(BF16)


def split3(x):
    high = x.astype(BF16)
    rest = x - high.astype(F32)
    mid = rest.astype(BF16)
    low = (rest - mid.astype(F32)).astype(BF16)
    return high, mid, low


def left4(x):
    h, m = split2(x)
    return jnp.concatenate([h, h, m, m], axis=1)


def right4(x):
    h, m = split2(x)
    return jnp.concatenate([h, m, h, m], axis=1)


def left6(x, axis=1):
    h, m, l = split3(x)
    return jnp.concatenate([h, h, m, h, m, l], axis=axis)


def right6(x, axis=1):
    h, m, l = split3(x)
    return jnp.concatenate([h, m, h, l, m, h], axis=axis)


def dot_nt(a, b):
    return lax.dot_general(a, b, (((1,), (1,)), ((), ())), preferred_element_type=F32)


def operand(points, is_left):
    h, m = split2(points)
    rounded = h.astype(F32) + m.astype(F32)
    half = -0.5 * jnp.sum(rounded * rounded, axis=1, keepdims=True)
    pieces = [jnp.broadcast_to(v.astype(F32), points.shape) for v in split3(half)]
    lane = lax.broadcasted_iota(jnp.int32, points.shape, 1)
    first = 3 if is_left else 0
    extra = jnp.where(lane < 6, 1.0, 0.0)
    for i, piece in enumerate(pieces):
        extra = jnp.where(lane == first + i, piece, extra)
    extra = extra.astype(BF16)
    if is_left:
        return jnp.concatenate([h, h, m, m, extra], axis=1)
    return jnp.concatenate([h, m, h, m, extra], axis=1)


def factor_inverse(w_ref, dv_ref):
    size = 16
    lane = lax.broadcasted_iota(jnp.int32, (size, B), 1)
    row = lax.broadcasted_iota(jnp.int32, (size, B), 0)

    def block(b, carry):
        start = pl.multiple_of(b * size, size)
        rows = pl.ds(start, size)
        left = w_ref[rows, 0:B]
        right = w_ref[rows, B : 2 * B]
        rolled = pltpu.roll(left, lax.rem(B - start, B), axis=1)
        cols = [jnp.broadcast_to(rolled[:, k : k + 1], (size, B)) for k in range(size)]
        inv = jnp.zeros((size, B), F32)
        for k in range(size):
            pivot = jnp.broadcast_to(cols[k][k : k + 1, :], (size, B))
            rinv = 1.0 / pivot
            inv = jnp.where(row == k, rinv, inv)
            mult = jnp.where(row > k, cols[k] * rinv, 0.0)
            for j in range(k + 1, size):
                cols[j] = cols[j] - mult * cols[j][k : k + 1, :]
            left = left - mult * left[k : k + 1, :]
            right = right - mult * right[k : k + 1, :]
        w_ref[rows, 0:B] = left
        w_ref[rows, B : 2 * B] = right
        dv_ref[rows, :] = inv
        scaled = jnp.where(lane >= start + size, left * inv, 0.0)
        update = lax.dot_general(
            left6(scaled, 0),
            right6(jnp.concatenate([left, right], axis=1), 0),
            (((0,), (0,)), ((), ())),
            preferred_element_type=F32,
        )
        w_ref[...] = w_ref[...] - update
        return carry

    lax.fori_loop(0, B // size, block, 0)
    return w_ref[:, B : 2 * B] * jnp.sqrt(dv_ref[...])


def gather_kernel(
    step_ref,
    feat_ref,
    ls_hbm,
    noise_hbm,
    comp_ref,
    covar_ref,
    mrow_ref,
    colc_ref,
    pf_ref,
    ls_ref,
    noise_ref,
    comp_v,
    feat_v,
    s_b,
    r_b,
    g_b,
    s_f,
    r_f,
    g_f,
    z_a,
    y_a,
    diag,
    colall,
    rowfeat,
    colcat,
    rowcat,
    rowc,
    w_v,
    dv_v,
    local_sem,
    send_sem,
    recv_sem,
):
    r = lax.axis_index("row")
    c = lax.axis_index("col")
    z = lax.rem(r, NZ)
    y = lax.div(r, NZ)
    axes = {
        "x": (c, NC, lambda i: (r, i)),
        "z": (z, NZ, lambda i: (y * NZ + i, c)),
        "y": (y, NY, lambda i: (i * NZ + z, c)),
    }
    partner = (y * NZ + c, z)
    far = {8: (4, 3, 5, 2, 6, 1, 7), 4: (2, 1, 3)}
    near = {8: (1, 7, 2, 6, 3, 5, 4), 4: (1, 3, 2)}

    def other(me, d, n):
        return lax.rem(me + d, n)

    feat_copy = pltpu.make_async_copy(feat_ref, feat_v, local_sem.at[0])
    comp_copy = pltpu.make_async_copy(comp_ref, comp_v, local_sem.at[1])
    ls_copy = pltpu.make_async_copy(ls_hbm, ls_ref, local_sem.at[2])
    noise_copy = pltpu.make_async_copy(noise_hbm, noise_ref, local_sem.at[3])
    comp_copy.start()
    feat_copy.start()
    ls_copy.start()
    noise_copy.start()

    barrier = pltpu.get_barrier_semaphore()
    for me, n, dev in axes.values():
        for d in far[n]:
            pl.semaphore_signal(barrier, inc=1, device_id=dev(other(me, d, n)), device_id_type=MESH)

    @pl.when(z != c)
    def _():
        pl.semaphore_signal(barrier, inc=1, device_id=partner, device_id_type=MESH)

    def remote(src, dst, send, recv, dev):
        return pltpu.make_async_remote_copy(
            src_ref=src,
            dst_ref=dst,
            send_sem=send_sem.at[send],
            recv_sem=recv_sem.at[recv],
            device_id=dev,
            device_id_type=MESH,
        )

    waits = []

    def spread(axis, src, dst, off, order=far):
        me, n, dev = axes[axis]
        for d in order[n]:
            peer = other(me, d, n)
            copy = remote(src(peer), dst(me), off + d, off + me, dev(peer))
            copy.start()
            waits.append(copy)

    def arrived(axis, dst, off, steps=None):
        me, n, dev = axes[axis]
        for d in steps or near[n]:
            peer = other(me, d, n)
            remote(dst(peer), dst(peer), off + d, off + peer, dev(peer)).wait_recv()

    p = step_ref[0]
    panel_m = lax.div(p, NC)
    panel_c = lax.rem(p, NC)
    panel_k = lax.div(p, NR)
    panel_r = lax.rem(p, NR)
    panel_z = lax.rem(panel_r, NZ)
    panel_y = lax.div(panel_r, NZ)
    comp_copy.wait()
    for k in range(KR):
        block = comp_v[pl.ds(k * (B * KC) + panel_m, B, stride=KC), :]
        s_b[:, k] = block.reshape(NC, PART, B)
    feat_copy.wait()
    ls_copy.wait()
    noise_copy.wait()
    inv_ls = 1.0 / ls_ref[...]
    feat_p = feat_v[lax.div(panel_m, 4), lax.rem(panel_m, 4)] * inv_ls
    s_f[:, 0:PART, :] = feat_p.reshape(NC, PART, B)
    noise_p = noise_ref[pl.ds(panel_m, 1), :]
    s_f[:, PART:FROWS, :] = jnp.broadcast_to(noise_p.reshape(1, 1, B), (NC, 8, B))
    r_b[c] = s_b[c]
    r_f[c] = s_f[c]

    @pl.when(z != c)
    def _():
        pl.semaphore_wait(barrier, 2 * NC + NY - 2)

    @pl.when(z == c)
    def _():
        pl.semaphore_wait(barrier, 2 * NC + NY - 3)

    spread("x", lambda i: s_b.at[i], lambda i: r_b.at[i], 0)
    spread("x", lambda i: s_f.at[i], lambda i: r_f.at[i], 8)

    feat_move = [remote(feat_v.at[k, y], rowfeat.at[k], 124 + k, 124 + k, partner) for k in range(KR)]

    @pl.when(z != c)
    def _():
        for copy in feat_move:
            copy.start()

    @pl.when(z == c)
    def _():
        for k in range(KR):
            rowfeat[k] = feat_v[k, y]

    def prepare(m, carry):
        pts = feat_v[lax.div(m, 4), lax.rem(m, 4)] * inv_ls
        colcat[pl.ds(pl.multiple_of(m * B, B), B), :] = operand(pts, False)
        return carry

    lax.fori_loop(0, KC, prepare, 0, unroll=4)

    arrived("x", lambda i: r_b.at[i], 0)
    g_b[c] = r_b[panel_c]
    move = remote(g_b.at[c], colall.at[y, c], 16, 16, partner)
    moved = remote(g_b.at[c], colall.at[y, z], 16, 16, partner)

    @pl.when(z != c)
    def _():
        move.start()

    @pl.when(z == c)
    def _():
        colall[y, z] = g_b[c]

    z_a[z] = r_b[panel_c, panel_k]
    spread("z", lambda i: z_a.at[z], lambda i: z_a.at[i], 20)
    spread("x", lambda i: g_b.at[c], lambda i: g_b.at[i], 28)
    arrived("x", lambda i: r_f.at[i], 8)
    g_f[c] = r_f[panel_c]
    spread("x", lambda i: g_f.at[c], lambda i: g_f.at[i], 36)

    @pl.when(z != c)
    def _():
        for copy in feat_move:
            copy.wait_recv()

    for k in range(KR):
        rowcat[k * B : (k + 1) * B, :] = operand(rowfeat[k] * inv_ls, True)
    eye = lax.broadcasted_iota(jnp.int32, (B, B), 0) == lax.broadcasted_iota(jnp.int32, (B, B), 1)

    def cover(part):
        for m2 in (2 * part, 2 * part + 1):
            expo = dot_nt(rowcat[...], colcat[m2 * 2 * B : (m2 + 1) * 2 * B, :])
            for j in range(2):
                m = m2 * 2 + j
                for k in range(KR):
                    value = jnp.exp(expo[k * B : (k + 1) * B, j * B : (j + 1) * B])
                    value = value + comp_v[pl.ds(k * (B * KC) + m, B, stride=KC), :]
                    if m // 4 == k:
                        same = jnp.logical_and(z == c, y == m % 4)
                        value = value + jnp.where(jnp.logical_and(eye, same), noise_ref[m : m + 1, :], 0.0)
                    covar_ref[m, k * B : (k + 1) * B, :] = value

    def forward(piece, slot):
        for d in near[NY]:
            peer = other(y, d, NY)
            copy = remote(
                colall.at[y, piece],
                colall.at[y, piece],
                60 + slot * 4 + d,
                92 + y * NZ + piece,
                axes["y"][2](peer),
            )
            copy.start()
            waits.append(copy)

    def relay(steps):
        for d in steps:
            arrived("z", lambda i: colall.at[y, i], 52, (d,))
            forward(other(z, d, NZ), d)

    arrived("z", lambda i: z_a.at[i], 20)
    y_a[y] = z_a[panel_z]
    spread("y", lambda i: y_a.at[y], lambda i: y_a.at[i], 44)

    @pl.when(z != c)
    def _():
        moved.wait_recv()

    spread("z", lambda i: colall.at[y, z], lambda i: colall.at[y, i], 52, near)
    forward(z, 0)
    cover(0)
    arrived("y", lambda i: y_a.at[i], 44)
    diag[c] = y_a[panel_y]
    spread("x", lambda i: diag.at[c], lambda i: diag.at[i], 128)
    relay((1, 7))
    cover(1)
    relay((2, 6))
    cover(2)
    relay((3, 5, 4))
    cover(3)

    arrived("x", lambda i: g_b.at[i], 28)
    arrived("x", lambda i: g_f.at[i], 36)
    pts_p = g_f[:, 0:PART, :].reshape(B, B)
    left_p, right_p = operand(pts_p, True), operand(pts_p, False)
    noise_p = jnp.where(eye, g_f[0, PART : PART + 1, :], 0.0)
    kernel_p = jnp.exp(dot_nt(left_p, right_p)) + noise_p
    kernel_row = jnp.exp(dot_nt(rowcat[...], right_p))
    for k in range(KR):
        here = k * NR + r == p
        raw = g_b[:, k].reshape(B, B)
        rowc[k * B : (k + 1) * B, :] = kernel_row[k * B : (k + 1) * B, :] + raw + jnp.where(here, noise_p, 0.0)

    arrived("x", lambda i: diag.at[i], 128)
    w_v[:, 0:B] = kernel_p + diag[...].reshape(B, B)
    w_v[:, B : 2 * B] = jnp.where(eye, 1.0, 0.0)
    linv = factor_inverse(w_v, dv_v)
    dv_v[...] = linv
    solved = dot_nt(left6(rowc[...]), right6(linv))
    weights = jnp.dot(left6(solved), right6(linv, 0), preferred_element_type=F32)
    share = right6(dv_v[pl.ds(pl.multiple_of(c * PART, PART), PART), :])
    mine = dot_nt(share, left6(rowc[...]))
    row = lax.broadcasted_iota(jnp.int32, (PART, B), 1)
    col = lax.broadcasted_iota(jnp.int32, (PART, B), 0) + c * PART
    for k in range(KR):
        w = k * NR + r
        mrow_ref[k * B : (k + 1) * B, :] = jnp.where(w > p, weights[k * B : (k + 1) * B, :], 0.0)
        keep = jnp.logical_or(w > p, jnp.logical_and(w == p, col <= row))
        pf_ref[k] = jnp.where(keep, mine[:, k * B : (k + 1) * B], 0.0)
    for m in range(KC):
        kern = jnp.exp(dot_nt(colcat[m * B : (m + 1) * B, :], left_p))
        colc_ref[m * B : (m + 1) * B, :] = kern

    for d in near[NY]:
        peer = other(y, d, NY)
        for piece in range(NZ):
            landed = colall.at[peer, piece]
            remote(landed, landed, 60, 92 + peer * NZ + piece, axes["y"][2](peer)).wait_recv()
    for m in range(KC):
        k, q = m // NY, m % NY
        raw = colall[q, :, k].reshape(B, B)
        rows = slice(m * B, (m + 1) * B)
        colc_ref[rows, :] = jnp.where(m * NC + c > p, colc_ref[rows, :] + raw, 0.0)

    for copy in waits:
        copy.wait_send()

    @pl.when(z != c)
    def _():
        move.wait_send()
        for copy in feat_move:
            copy.wait_send()


def update_kernel(covar_ref, mrow_ref, colc_ref, pf_in, out_ref, pf_ref, out_v, sem):
    left = left4(mrow_ref[...])
    copies = []
    for half in range(2):
        for pair in range(2):
            rows = slice(pair * 2 * B, (pair + 1) * 2 * B)
            for m2 in range(half * 4, half * 4 + 4):
                update = dot_nt(left[rows, :], right4(colc_ref[m2 * 2 * B : (m2 + 1) * 2 * B, :]))
                for j in range(2):
                    m = m2 * 2 + j
                    value = covar_ref[m, rows, :] - update[:, j * B : (j + 1) * B]
                    out_v[pl.ds(pair * 2 * B * KC + m, 2 * B, stride=KC), :] = value
            view = out_v.reshape(KR * B, KC, B)
            part = (pl.ds(pair * 2 * B, 2 * B), pl.ds(half * 8, 8))
            copy = pltpu.make_async_copy(view.at[part], out_ref.at[part], sem.at[half * 2 + pair])
            copy.start()
            copies.append(copy)
    pf_ref[...] = pf_in[...]
    for copy in copies:
        copy.wait()


def in_hbm(x):
    return pltpu.with_memory_space_constraint(x, pltpu.HBM)


def body(features, lengthscales, noise_var, component, step_index):
    hbm = pl.BlockSpec(memory_space=pltpu.HBM)
    vmem = pl.BlockSpec(memory_space=pltpu.VMEM)
    smem = pl.BlockSpec(memory_space=pltpu.SMEM)
    covar, mrow, colc, pf = pl.pallas_call(
        gather_kernel,
        out_shape=(
            jax.ShapeDtypeStruct((KC, KR * B, B), F32),
            jax.ShapeDtypeStruct((KR * B, B), F32),
            jax.ShapeDtypeStruct((KC * B, B), F32),
            jax.ShapeDtypeStruct((KR, PART, B), F32),
        ),
        in_specs=[smem, hbm, hbm, hbm, hbm],
        out_specs=(vmem, vmem, vmem, vmem),
        scratch_shapes=[
            pltpu.VMEM((1, B), F32),
            pltpu.VMEM((KC, B), F32),
            pltpu.VMEM((KR * B * KC, B), F32),
            pltpu.VMEM((4, 4, B, B), F32),
            pltpu.VMEM((NC, KR, PART, B), F32),
            pltpu.VMEM((NC, KR, PART, B), F32),
            pltpu.VMEM((NC, KR, PART, B), F32),
            pltpu.VMEM((NC, FROWS, B), F32),
            pltpu.VMEM((NC, FROWS, B), F32),
            pltpu.VMEM((NC, FROWS, B), F32),
            pltpu.VMEM((NZ, PART, B), F32),
            pltpu.VMEM((NY, PART, B), F32),
            pltpu.VMEM((NC, PART, B), F32),
            pltpu.VMEM((NY, NZ, KR, PART, B), F32),
            pltpu.VMEM((KR, B, B), F32),
            pltpu.VMEM((KC * B, DEPTH), BF16),
            pltpu.VMEM((KR * B, DEPTH), BF16),
            pltpu.VMEM((KR * B, B), F32),
            pltpu.VMEM((B, 2 * B), F32),
            pltpu.VMEM((B, B), F32),
            pltpu.SemaphoreType.DMA((4,)),
            pltpu.SemaphoreType.DMA((136,)),
            pltpu.SemaphoreType.DMA((136,)),
        ],
        compiler_params=pltpu.CompilerParams(
            collective_id=0, has_side_effects=True, vmem_limit_bytes=GATHER_VMEM
        ),
        name="gather_panel",
    )(
        step_index,
        in_hbm(features.reshape(4, 4, B, B)),
        in_hbm(lengthscales.reshape(1, B)),
        in_hbm(noise_var),
        in_hbm(component.reshape(KR * B * KC, B)),
    )
    trailing, pf = pl.pallas_call(
        update_kernel,
        out_shape=(
            jax.ShapeDtypeStruct((KR * B, KC, B), F32),
            jax.ShapeDtypeStruct((KR, PART, B), F32),
        ),
        in_specs=[vmem, vmem, vmem, vmem],
        out_specs=(hbm, vmem),
        scratch_shapes=[
            pltpu.VMEM((KR * B * KC, B), F32),
            pltpu.SemaphoreType.DMA((4,)),
        ],
        compiler_params=pltpu.CompilerParams(vmem_limit_bytes=UPDATE_VMEM),
        name="update_blocks",
    )(covar, mrow, colc, pf)
    return jnp.swapaxes(pf, 1, 2), trailing.reshape(KR, B, KC, B)


def solution(mesh):
    in_specs = (P(None, "col", None), P(), P(None, "col"), P(None, "row", None, "col"), P())
    out_specs = (P(None, "row", "col"), P(None, "row", None, "col"))
    return jax.shard_map(body, mesh=mesh, in_specs=in_specs, out_specs=out_specs, check_vma=False)
```

time: 74.4 us -> 57.1 us (0.77)
  the two profiles are of different devices: /device:TPU:3 before, /device:TPU:1 now
where the time goes in v2:
time: 57.1 us; the launch traced here: 57 us
  Pallas kernels  55.7 us (98%)
  between operations  1.29 us (2%)
    pallas_call x1, Pallas kernels, body(): pl.pallas_call(gather_kernel, out_shape=(jax.ShapeDtypeStruct((KC, KR * B...  52 us
    pallas_call x1, Pallas kernels, body(): pl.pallas_call(update_kernel, out_shape=(jax.ShapeDtypeStruct((KR * B, KC...  3.64 us

profile of v2, /device:TPU:1, one launch (start us, length us, event | category | flops | bytes accessed | tf_op | source)
XLA Modules:
  0.0 57.0 jit_solution(14130184763702635226)
XLA Ops:
  1.3 52.0 %gather_panel.1 = (f32[16,512,128]{2,1,0:T(8,128)S(1)}, f32[512,128]{1,0:T(8,128)S(1)}, f32[2048,128]{1,0:T(8,128)S(1)}, f32[4,16,128]{2,1,0:T(8,128)S(1)}) custom-call(s32[1]{0:T(128)S(6)} %copy.7.step_ref, f32[4,4,128,128]{3,2,1,0:T(8,128)} %bitcast.6, f32[1,128]{1,0:T(1,128)} %bitcast.7, f32[16,128]{1,0:T(8,128)} %noise_hbm.1, f32[8192,128]{1,0:T(8,128)} %bitcast.5), custom_call_target="tpu_custom_call" | custom-call | tf_op jit(solution)/shard_map/gather_panel/pallas_call | solution.py:426
  53.3 3.6 %update_blocks.1 = (f32[512,16,128]{2,1,0:T(8,128)}, f32[4,16,128]{2,1,0:T(8,128)}) custom-call(f32[16,512,128]{2,1,0:T(8,128)S(1)} %get-tuple-element.8.covar_ref, f32[512,128]{1,0:T(8,128)S(1)} %get-tuple-element.9.mrow_ref, f32[2048,128]{1,0:T(8,128)S(1)} %get-tuple-element.10.colc_ref, f32[4,16,128]{2,1,0:T(8,128)S(1)} %get-tuple-element.11.pf_in), custom_call_target="tpu_custom_call" | custom-call | tf_op jit(solution)/shard_map/update_blocks/pallas_call | solution.py:472

commit v3 on v2

--- a/solution.py
+++ b/solution.py
@@ -14,8 +14,7 @@
 KR, KC, NR, NC = 4, 16, 32, 8
 NY, NZ = 4, 8
 PART = B // NC
-PANEL = KR * PART
-FROWS = PART + 8
+GROUP = 2 * KR + 2
 DEPTH = 5 * B
 GATHER_VMEM = 40 * 1024 * 1024
 UPDATE_VMEM = 16 * 1024 * 1024
@@ -125,19 +124,23 @@
     pf_ref,
     ls_ref,
     noise_ref,
-    comp_v,
+    comp_0,
+    comp_1,
+    comp_2,
+    comp_3,
     feat_v,
+    s_a,
+    r_a,
     s_b,
     r_b,
-    g_b,
     s_f,
     r_f,
-    g_f,
+    group,
     z_a,
     y_a,
     diag,
-    colall,
-    rowfeat,
+    ybuf,
+    xbuf,
     colcat,
     rowcat,
     rowc,
@@ -157,17 +160,23 @@
         "y": (y, NY, lambda i: (i * NZ + z, c)),
     }
     partner = (y * NZ + c, z)
+    sibling = c + 1 - 2 * lax.rem(c, 2)
     far = {8: (4, 3, 5, 2, 6, 1, 7), 4: (2, 1, 3)}
     near = {8: (1, 7, 2, 6, 3, 5, 4), 4: (1, 3, 2)}
 
     def other(me, d, n):
         return lax.rem(me + d, n)
 
+    comp_v = (comp_0, comp_1, comp_2, comp_3)
+    comp_copies = [
+        pltpu.make_async_copy(comp_ref.at[pl.ds(k * B * KC, B * KC)], comp_v[k], local_sem.at[4 + k])
+        for k in range(KR)
+    ]
     feat_copy = pltpu.make_async_copy(feat_ref, feat_v, local_sem.at[0])
-    comp_copy = pltpu.make_async_copy(comp_ref, comp_v, local_sem.at[1])
-    ls_copy = pltpu.make_async_copy(ls_hbm, ls_ref, local_sem.at[2])
-    noise_copy = pltpu.make_async_copy(noise_hbm, noise_ref, local_sem.at[3])
-    comp_copy.start()
+    ls_copy = pltpu.make_async_copy(ls_hbm, ls_ref, local_sem.at[1])
+    noise_copy = pltpu.make_async_copy(noise_hbm, noise_ref, local_sem.at[2])
+    for copy in comp_copies:
+        copy.start()
     feat_copy.start()
     ls_copy.start()
     noise_copy.start()
@@ -193,13 +202,15 @@
 
     waits = []
 
+    def post(copy):
+        copy.start()
+        waits.append(copy)
+
     def spread(axis, src, dst, off, order=far):
         me, n, dev = axes[axis]
         for d in order[n]:
             peer = other(me, d, n)
-            copy = remote(src(peer), dst(me), off + d, off + me, dev(peer))
-            copy.start()
-            waits.append(copy)
+            post(remote(src(peer), dst(me), off + d, off + me, dev(peer)))
 
     def arrived(axis, dst, off, steps=None):
         me, n, dev = axes[axis]
@@ -214,145 +225,191 @@
     panel_r = lax.rem(p, NR)
     panel_z = lax.rem(panel_r, NZ)
     panel_y = lax.div(panel_r, NZ)
-    comp_copy.wait()
+
     for k in range(KR):
-        block = comp_v[pl.ds(k * (B * KC) + panel_m, B, stride=KC), :]
+        comp_copies[k].wait()
+        block = comp_v[k][pl.ds(panel_m, B, stride=KC), :]
         s_b[:, k] = block.reshape(NC, PART, B)
+    s_a[...] = s_b[:, panel_k]
+    r_a[c] = s_a[c]
+    r_b[c] = s_b[c]
+
+    @pl.when(z != c)
+    def _():
+        pl.semaphore_wait(barrier, 2 * NC + NY - 2)
+
+    @pl.when(z == c)
+    def _():
+        pl.semaphore_wait(barrier, 2 * NC + NY - 3)
+
+    spread("x", lambda i: s_a.at[i], lambda i: r_a.at[i], 0)
+    spread("x", lambda i: s_b.at[i], lambda i: r_b.at[i], 8)
     feat_copy.wait()
     ls_copy.wait()
     noise_copy.wait()
+
+    part = pl.ds(pl.multiple_of(z * PART, PART), PART)
+    feat_out = remote(feat_v.at[:, y, part, :], group.at[z, 6:10], 24, 24, partner)
+    feat_in = remote(feat_v.at[:, y, part, :], group.at[c, 6:10], 24, 24, partner)
+
+    @pl.when(z != c)
+    def _():
+        feat_out.start()
+
+    @pl.when(z == c)
+    def _():
+        for k in range(KR):
+            group[c, 6 + k] = feat_v[k, y, part, :]
+
     inv_ls = 1.0 / ls_ref[...]
     feat_p = feat_v[lax.div(panel_m, 4), lax.rem(panel_m, 4)] * inv_ls
-    s_f[:, 0:PART, :] = feat_p.reshape(NC, PART, B)
+    s_f[:, 0] = feat_p.reshape(NC, PART, B)
     noise_p = noise_ref[pl.ds(panel_m, 1), :]
-    s_f[:, PART:FROWS, :] = jnp.broadcast_to(noise_p.reshape(1, 1, B), (NC, 8, B))
-    r_b[c] = s_b[c]
+    s_f[:, 1] = jnp.broadcast_to(noise_p.reshape(1, 1, B), (NC, PART, B))
     r_f[c] = s_f[c]
-
-    @pl.when(z != c)
-    def _():
-        pl.semaphore_wait(barrier, 2 * NC + NY - 2)
-
-    @pl.when(z == c)
-    def _():
-        pl.semaphore_wait(barrier, 2 * NC + NY - 3)
-
-    spread("x", lambda i: s_b.at[i], lambda i: r_b.at[i], 0)
-    spread("x", lambda i: s_f.at[i], lambda i: r_f.at[i], 8)
-
-    feat_move = [remote(feat_v.at[k, y], rowfeat.at[k], 124 + k, 124 + k, partner) for k in range(KR)]
-
-    @pl.when(z != c)
-    def _():
-        for copy in feat_move:
-            copy.start()
-
-    @pl.when(z == c)
-    def _():
-        for k in range(KR):
-            rowfeat[k] = feat_v[k, y]
+    spread("x", lambda i: s_f.at[i], lambda i: r_f.at[i], 16)
 
     def prepare(m, carry):
         pts = feat_v[lax.div(m, 4), lax.rem(m, 4)] * inv_ls
         colcat[pl.ds(pl.multiple_of(m * B, B), B), :] = operand(pts, False)
         return carry
 
-    lax.fori_loop(0, KC, prepare, 0, unroll=4)
-
-    arrived("x", lambda i: r_b.at[i], 0)
-    g_b[c] = r_b[panel_c]
-    move = remote(g_b.at[c], colall.at[y, c], 16, 16, partner)
-    moved = remote(g_b.at[c], colall.at[y, z], 16, 16, partner)
+    lax.fori_loop(0, KC // 2, prepare, 0, unroll=4)
+
+    arrived("x", lambda i: r_a.at[i], 0)
+    z_a[z] = r_a[panel_c]
+    spread("z", lambda i: z_a.at[z], lambda i: z_a.at[i], 32)
+
+    def over_y(rel):
+        for d in near[NY]:
+            peer = other(y, d, NY)
+            slot = NY - d
+            send = remote(
+                ybuf.at[rel, 0], ybuf.at[rel, slot], 64 + rel * 4 + d, 64 + rel * 4 + slot, axes["y"][2](peer)
+            )
+            post(send)
+
+    def from_y(rel):
+        for d in near[NY]:
+            peer = other(y, d, NY)
+            here = ybuf.at[rel, d]
+            remote(here, here, 64, 64 + rel * 4 + d, axes["y"][2](peer)).wait_recv()
+
+    over_x_waits = []
+
+    def over_x(rel, first, count, off):
+        target = other(z, rel, NZ)
+        src = ybuf.at[rel, first : first + count]
+        dst = xbuf.at[c, first : first + count]
+        send = remote(src, dst, off + rel, off + c, (r, target))
+        here = pltpu.make_async_copy(src, dst, send_sem.at[off + rel])
+
+        @pl.when(target != c)
+        def _():
+            send.start()
+
+        @pl.when(target == c)
+        def _():
+            here.start()
+
+        over_x_waits.append((target, send, here))
+
+    arrived("x", lambda i: r_b.at[i], 8)
+    ybuf[0, 0] = r_b[panel_c]
+    group[c, 0:4] = r_b[panel_c]
+    for d in near[NZ]:
+        peer = other(z, d, NZ)
+        post(remote(ybuf.at[0, 0], ybuf.at[NZ - d, 0], 40 + d, 40 + NZ - d, axes["z"][2](peer)))
+    over_y(0)
+    over_x(0, 0, 1, 96)
+
+    def relay(steps):
+        for d in steps:
+            here = ybuf.at[d, 0]
+            remote(here, here, 40, 40 + d, axes["z"][2](other(z, d, NZ))).wait_recv()
+            over_y(d)
+            over_x(d, 0, 1, 96)
+
+    lax.fori_loop(KC // 2, KC, prepare, 0, unroll=4)
+    relay((1, 7))
+
+    arrived("x", lambda i: r_f.at[i], 16)
+    group[c, 4:6] = r_f[panel_c]
 
     @pl.when(z != c)
     def _():
-        move.start()
-
-    @pl.when(z == c)
-    def _():
-        colall[y, z] = g_b[c]
-
-    z_a[z] = r_b[panel_c, panel_k]
-    spread("z", lambda i: z_a.at[z], lambda i: z_a.at[i], 20)
-    spread("x", lambda i: g_b.at[c], lambda i: g_b.at[i], 28)
-    arrived("x", lambda i: r_f.at[i], 8)
-    g_f[c] = r_f[panel_c]
-    spread("x", lambda i: g_f.at[c], lambda i: g_f.at[i], 36)
-
-    @pl.when(z != c)
-    def _():
-        for copy in feat_move:
-            copy.wait_recv()
+        feat_in.wait_recv()
+
+    mates = [(0, sibling)] + [(d, other(c, d, NC)) for d in (2, 6, 4)]
+    for d, peer in mates[1:] + mates[:1]:
+        post(remote(group.at[c], group.at[c], 112 + d, 112 + c, (r, peer)))
+
+    arrived("z", lambda i: z_a.at[i], 32)
+    y_a[y] = z_a[panel_z]
+    spread("y", lambda i: y_a.at[y], lambda i: y_a.at[i], 48)
+    relay((2, 6))
+    from_y(0)
+    over_x(0, 1, 3, 104)
+
+    for d, peer in mates[1:]:
+        slot = group.at[peer]
+        remote(slot, slot, 112 + d, 112 + peer, (r, peer)).wait_recv()
+        post(remote(slot, slot, 113 + d, 112 + peer, (r, sibling)))
+
+    arrived("y", lambda i: y_a.at[i], 48)
+    diag[c] = y_a[panel_y]
+    spread("x", lambda i: diag.at[c], lambda i: diag.at[i], 56)
+    relay((3, 5))
+    for d in (1, 7):
+        from_y(d)
+        over_x(d, 1, 3, 104)
+    for d in (0, 2, 6, 4):
+        slot = group.at[other(sibling, d, NC)]
+        remote(slot, slot, 112, 112 + other(sibling, d, NC), (r, sibling)).wait_recv()
 
     for k in range(KR):
-        rowcat[k * B : (k + 1) * B, :] = operand(rowfeat[k] * inv_ls, True)
+        rows = group[:, 6 + k].reshape(B, B)
+        rowcat[k * B : (k + 1) * B, :] = operand(rows * inv_ls, True)
     eye = lax.broadcasted_iota(jnp.int32, (B, B), 0) == lax.broadcasted_iota(jnp.int32, (B, B), 1)
 
-    def cover(part):
-        for m2 in (2 * part, 2 * part + 1):
+    def cover(quarter):
+        for m2 in (2 * quarter, 2 * quarter + 1):
             expo = dot_nt(rowcat[...], colcat[m2 * 2 * B : (m2 + 1) * 2 * B, :])
             for j in range(2):
                 m = m2 * 2 + j
                 for k in range(KR):
                     value = jnp.exp(expo[k * B : (k + 1) * B, j * B : (j + 1) * B])
-                    value = value + comp_v[pl.ds(k * (B * KC) + m, B, stride=KC), :]
+                    value = value + comp_v[k][pl.ds(m, B, stride=KC), :]
                     if m // 4 == k:
                         same = jnp.logical_and(z == c, y == m % 4)
                         value = value + jnp.where(jnp.logical_and(eye, same), noise_ref[m : m + 1, :], 0.0)
                     covar_ref[m, k * B : (k + 1) * B, :] = value
 
-    def forward(piece, slot):
-        for d in near[NY]:
-            peer = other(y, d, NY)
-            copy = remote(
-                colall.at[y, piece],
-                colall.at[y, piece],
-                60 + slot * 4 + d,
-                92 + y * NZ + piece,
-                axes["y"][2](peer),
-            )
-            copy.start()
-            waits.append(copy)
-
-    def relay(steps):
-        for d in steps:
-            arrived("z", lambda i: colall.at[y, i], 52, (d,))
-            forward(other(z, d, NZ), d)
-
-    arrived("z", lambda i: z_a.at[i], 20)
-    y_a[y] = z_a[panel_z]
-    spread("y", lambda i: y_a.at[y], lambda i: y_a.at[i], 44)
-
-    @pl.when(z != c)
-    def _():
-        moved.wait_recv()
-
-    spread("z", lambda i: colall.at[y, z], lambda i: colall.at[y, i], 52, near)
-    forward(z, 0)
     cover(0)
-    arrived("y", lambda i: y_a.at[i], 44)
-    diag[c] = y_a[panel_y]
-    spread("x", lambda i: diag.at[c], lambda i: diag.at[i], 128)
-    relay((1, 7))
+    relay((4,))
+    for d in (2, 6):
+        from_y(d)
+        over_x(d, 1, 3, 104)
     cover(1)
-    relay((2, 6))
+    for d in (3, 5):
+        from_y(d)
+        over_x(d, 1, 3, 104)
     cover(2)
-    relay((3, 5, 4))
+    from_y(4)
+    over_x(4, 1, 3, 104)
     cover(3)
 
-    arrived("x", lambda i: g_b.at[i], 28)
-    arrived("x", lambda i: g_f.at[i], 36)
-    pts_p = g_f[:, 0:PART, :].reshape(B, B)
+    pts_p = group[:, 4].reshape(B, B)
     left_p, right_p = operand(pts_p, True), operand(pts_p, False)
-    noise_p = jnp.where(eye, g_f[0, PART : PART + 1, :], 0.0)
+    noise_p = jnp.where(eye, group[0, 5, 0:1, :], 0.0)
     kernel_p = jnp.exp(dot_nt(left_p, right_p)) + noise_p
     kernel_row = jnp.exp(dot_nt(rowcat[...], right_p))
     for k in range(KR):
         here = k * NR + r == p
-        raw = g_b[:, k].reshape(B, B)
+        raw = group[:, k].reshape(B, B)
         rowc[k * B : (k + 1) * B, :] = kernel_row[k * B : (k + 1) * B, :] + raw + jnp.where(here, noise_p, 0.0)
 
-    arrived("x", lambda i: diag.at[i], 128)
+    arrived("x", lambda i: diag.at[i], 56)
     w_v[:, 0:B] = kernel_p + diag[...].reshape(B, B)
     w_v[:, B : 2 * B] = jnp.where(eye, 1.0, 0.0)
     linv = factor_inverse(w_v, dv_v)
@@ -368,29 +425,42 @@
         mrow_ref[k * B : (k + 1) * B, :] = jnp.where(w > p, weights[k * B : (k + 1) * B, :], 0.0)
         keep = jnp.logical_or(w > p, jnp.logical_and(w == p, col <= row))
         pf_ref[k] = jnp.where(keep, mine[:, k * B : (k + 1) * B], 0.0)
-    for m in range(KC):
-        kern = jnp.exp(dot_nt(colcat[m * B : (m + 1) * B, :], left_p))
-        colc_ref[m * B : (m + 1) * B, :] = kern
-
-    for d in near[NY]:
-        peer = other(y, d, NY)
-        for piece in range(NZ):
-            landed = colall.at[peer, piece]
-            remote(landed, landed, 60, 92 + peer * NZ + piece, axes["y"][2](peer)).wait_recv()
-    for m in range(KC):
-        k, q = m // NY, m % NY
-        raw = colall[q, :, k].reshape(B, B)
-        rows = slice(m * B, (m + 1) * B)
-        colc_ref[rows, :] = jnp.where(m * NC + c > p, colc_ref[rows, :] + raw, 0.0)
+
+    def column(m, carry):
+        rows = pl.ds(pl.multiple_of(m * B, B), B)
+        colc_ref[rows, :] = jnp.exp(dot_nt(colcat[rows, :], left_p))
+        return carry
+
+    lax.fori_loop(0, KC, column, 0, unroll=8)
+
+    for target, send, here in over_x_waits:
+
+        @pl.when(target != c)
+        def _(send=send):
+            send.wait_send()
+
+        @pl.when(target == c)
+        def _(here=here):
+            here.wait()
+
+    for d in near[NC]:
+        peer = other(c, d, NC)
+        for off, first, count in ((96, 0, 1), (104, 1, 3)):
+            here = xbuf.at[peer, first : first + count]
+            remote(here, here, off, off + peer, (r, peer)).wait_recv()
+    for rel in range(NY):
+        for k in range(KR):
+            m = k * 4 + other(y, rel, NY)
+            raw = xbuf[:, rel, k].reshape(B, B)
+            rows = pl.ds(pl.multiple_of(m * B, B), B)
+            colc_ref[rows, :] = jnp.where(m * NC + c > p, colc_ref[rows, :] + raw, 0.0)
 
     for copy in waits:
         copy.wait_send()
 
     @pl.when(z != c)
     def _():
-        move.wait_send()
-        for copy in feat_move:
-            copy.wait_send()
+        feat_out.wait_send()
 
 
 def update_kernel(covar_ref, mrow_ref, colc_ref, pf_in, out_ref, pf_ref, out_v, sem):
@@ -436,25 +506,29 @@
         scratch_shapes=[
             pltpu.VMEM((1, B), F32),
             pltpu.VMEM((KC, B), F32),
-            pltpu.VMEM((KR * B * KC, B), F32),
+            pltpu.VMEM((B * KC, B), F32),
+            pltpu.VMEM((B * KC, B), F32),
+            pltpu.VMEM((B * KC, B), F32),
+            pltpu.VMEM((B * KC, B), F32),
             pltpu.VMEM((4, 4, B, B), F32),
+            pltpu.VMEM((NC, PART, B), F32),
+            pltpu.VMEM((NC, PART, B), F32),
             pltpu.VMEM((NC, KR, PART, B), F32),
             pltpu.VMEM((NC, KR, PART, B), F32),
-            pltpu.VMEM((NC, KR, PART, B), F32),
-            pltpu.VMEM((NC, FROWS, B), F32),
-            pltpu.VMEM((NC, FROWS, B), F32),
-            pltpu.VMEM((NC, FROWS, B), F32),
+            pltpu.VMEM((NC, 2, PART, B), F32),
+            pltpu.VMEM((NC, 2, PART, B), F32),
+            pltpu.VMEM((NC, GROUP, PART, B), F32),
             pltpu.VMEM((NZ, PART, B), F32),
             pltpu.VMEM((NY, PART, B), F32),
             pltpu.VMEM((NC, PART, B), F32),
-            pltpu.VMEM((NY, NZ, KR, PART, B), F32),
-            pltpu.VMEM((KR, B, B), F32),
+            pltpu.VMEM((NZ, NY, KR, PART, B), F32),
+            pltpu.VMEM((NC, NY, KR, PART, B), F32),
             pltpu.VMEM((KC * B, DEPTH), BF16),
             pltpu.VMEM((KR * B, DEPTH), BF16),
             pltpu.VMEM((KR * B, B), F32),
             pltpu.VMEM((B, 2 * B), F32),
             pltpu.VMEM((B, B), F32),
-            pltpu.SemaphoreType.DMA((4,)),
+            pltpu.SemaphoreType.DMA((8,)),
             pltpu.SemaphoreType.DMA((136,)),
             pltpu.SemaphoreType.DMA((136,)),
         ],

time: 57.1 us -> 50.5 us (0.88)
  Pallas kernels: 55.7 us -> 49.1 us
    pallas_call x1, Pallas kernels: 52 us -> 45.5 us  [body(): pl.pallas_call(gather_kernel, out_shape=(jax.ShapeDtypeStruct((KC, KR * B...]
where the time goes in v3:
time: 50.5 us; the launch traced here: 50.4 us
  Pallas kernels  49.1 us (97%)
  between operations  1.29 us (3%)
    pallas_call x1, Pallas kernels, body(): pl.pallas_call(gather_kernel, out_shape=(jax.ShapeDtypeStruct((KC, KR * B...  45.5 us
    pallas_call x1, Pallas kernels, body(): pl.pallas_call(update_kernel, out_shape=(jax.ShapeDtypeStruct((KR * B, KC...  3.63 us

profile of v3, /device:TPU:1, one launch (start us, length us, event | category | flops | bytes accessed | tf_op | source)
XLA Modules:
  0.0 50.4 jit_solution(10856003566366699092)
XLA Ops:
  1.3 45.5 %gather_panel.1 = (f32[16,512,128]{2,1,0:T(8,128)S(1)}, f32[512,128]{1,0:T(8,128)S(1)}, f32[2048,128]{1,0:T(8,128)S(1)}, f32[4,16,128]{2,1,0:T(8,128)S(1)}) custom-call(s32[1]{0:T(128)S(6)} %copy.7.step_ref, f32[4,4,128,128]{3,2,1,0:T(8,128)} %bitcast.6, f32[1,128]{1,0:T(1,128)} %bitcast.7, f32[16,128]{1,0:T(8,128)} %noise_hbm.1, f32[8192,128]{1,0:T(8,128)} %bitcast.5), custom_call_target="tpu_custom_call" | custom-call | tf_op jit(solution)/shard_map/gather_panel/pallas_call | solution.py:496
  46.7 3.6 %update_blocks.1 = (f32[512,16,128]{2,1,0:T(8,128)}, f32[4,16,128]{2,1,0:T(8,128)}) custom-call(f32[16,512,128]{2,1,0:T(8,128)S(1)} %get-tuple-element.8.covar_ref, f32[512,128]{1,0:T(8,128)S(1)} %get-tuple-element.9.mrow_ref, f32[2048,128]{1,0:T(8,128)S(1)} %get-tuple-element.10.colc_ref, f32[4,16,128]{2,1,0:T(8,128)S(1)} %get-tuple-element.11.pf_in), custom_call_target="tpu_custom_call" | custom-call | tf_op jit(solution)/shard_map/update_blocks/pallas_call | solution.py:546

commit v4 on v3

--- a/solution.py
+++ b/solution.py
@@ -73,7 +73,7 @@
     return jnp.concatenate([h, m, h, m, extra], axis=1)
 
 
-def factor_inverse(w_ref, dv_ref):
+def eliminate(w_ref, dv_ref, first, last):
     size = 16
     lane = lax.broadcasted_iota(jnp.int32, (size, B), 1)
     row = lax.broadcasted_iota(jnp.int32, (size, B), 0)
@@ -108,8 +108,7 @@
         w_ref[...] = w_ref[...] - update
         return carry
 
-    lax.fori_loop(0, B // size, block, 0)
-    return w_ref[:, B : 2 * B] * jnp.sqrt(dv_ref[...])
+    lax.fori_loop(first, last, block, 0)
 
 
 def gather_kernel(
@@ -140,7 +139,6 @@
     y_a,
     diag,
     ybuf,
-    xbuf,
     colcat,
     rowcat,
     rowc,
@@ -280,6 +278,18 @@
     z_a[z] = r_a[panel_c]
     spread("z", lambda i: z_a.at[z], lambda i: z_a.at[i], 32)
 
+    arrived("x", lambda i: r_b.at[i], 8)
+    group[c, 0:4] = r_b[panel_c]
+    move = remote(group.at[c, 0:4], ybuf.at[0, 0], 25, 25, partner)
+
+    @pl.when(z != c)
+    def _():
+        move.start()
+
+    @pl.when(z == c)
+    def _():
+        ybuf[0, 0] = group[c, 0:4]
+
     def over_y(rel):
         for d in near[NY]:
             peer = other(y, d, NY)
@@ -295,43 +305,24 @@
             here = ybuf.at[rel, d]
             remote(here, here, 64, 64 + rel * 4 + d, axes["y"][2](peer)).wait_recv()
 
-    over_x_waits = []
-
-    def over_x(rel, first, count, off):
-        target = other(z, rel, NZ)
-        src = ybuf.at[rel, first : first + count]
-        dst = xbuf.at[c, first : first + count]
-        send = remote(src, dst, off + rel, off + c, (r, target))
-        here = pltpu.make_async_copy(src, dst, send_sem.at[off + rel])
-
-        @pl.when(target != c)
-        def _():
-            send.start()
-
-        @pl.when(target == c)
-        def _():
-            here.start()
-
-        over_x_waits.append((target, send, here))
-
-    arrived("x", lambda i: r_b.at[i], 8)
-    ybuf[0, 0] = r_b[panel_c]
-    group[c, 0:4] = r_b[panel_c]
-    for d in near[NZ]:
+    def over_z(d, quarter):
         peer = other(z, d, NZ)
-        post(remote(ybuf.at[0, 0], ybuf.at[NZ - d, 0], 40 + d, 40 + NZ - d, axes["z"][2](peer)))
-    over_y(0)
-    over_x(0, 0, 1, 96)
+        sem = 40 if quarter == 0 else 96 + 8 * (quarter - 1)
+        post(
+            remote(
+                ybuf.at[0, quarter], ybuf.at[NZ - d, quarter], sem + d, sem + NZ - d, axes["z"][2](peer)
+            )
+        )
+
+    def from_z(d, quarter):
+        here = ybuf.at[d, quarter]
+        sem = 40 if quarter == 0 else 96 + 8 * (quarter - 1)
+        remote(here, here, sem, sem + d, axes["z"][2](other(z, d, NZ))).wait_recv()
 
     def relay(steps):
         for d in steps:
-            here = ybuf.at[d, 0]
-            remote(here, here, 40, 40 + d, axes["z"][2](other(z, d, NZ))).wait_recv()
+            from_z(d, 0)
             over_y(d)
-            over_x(d, 0, 1, 96)
-
-    lax.fori_loop(KC // 2, KC, prepare, 0, unroll=4)
-    relay((1, 7))
 
     arrived("x", lambda i: r_f.at[i], 16)
     group[c, 4:6] = r_f[panel_c]
@@ -342,30 +333,35 @@
 
     mates = [(0, sibling)] + [(d, other(c, d, NC)) for d in (2, 6, 4)]
     for d, peer in mates[1:] + mates[:1]:
-        post(remote(group.at[c], group.at[c], 112 + d, 112 + c, (r, peer)))
+        post(remote(group.at[c], group.at[c], 120 + d, 120 + c, (r, peer)))
+    lax.fori_loop(KC // 2, KC, prepare, 0, unroll=4)
 
     arrived("z", lambda i: z_a.at[i], 32)
     y_a[y] = z_a[panel_z]
     spread("y", lambda i: y_a.at[y], lambda i: y_a.at[i], 48)
-    relay((2, 6))
-    from_y(0)
-    over_x(0, 1, 3, 104)
 
     for d, peer in mates[1:]:
         slot = group.at[peer]
-        remote(slot, slot, 112 + d, 112 + peer, (r, peer)).wait_recv()
-        post(remote(slot, slot, 113 + d, 112 + peer, (r, sibling)))
+        remote(slot, slot, 120 + d, 120 + peer, (r, peer)).wait_recv()
+        post(remote(slot, slot, 121 + d, 120 + peer, (r, sibling)))
 
     arrived("y", lambda i: y_a.at[i], 48)
     diag[c] = y_a[panel_y]
     spread("x", lambda i: diag.at[c], lambda i: diag.at[i], 56)
-    relay((3, 5))
-    for d in (1, 7):
-        from_y(d)
-        over_x(d, 1, 3, 104)
+
+    @pl.when(z != c)
+    def _():
+        move.wait_recv()
+
+    for d in near[NZ][:4]:
+        over_z(d, 0)
+    over_y(0)
+    for d in near[NZ][4:]:
+        over_z(d, 0)
+
     for d in (0, 2, 6, 4):
         slot = group.at[other(sibling, d, NC)]
-        remote(slot, slot, 112, 112 + other(sibling, d, NC), (r, sibling)).wait_recv()
+        remote(slot, slot, 120, 120 + other(sibling, d, NC), (r, sibling)).wait_recv()
 
     for k in range(KR):
         rows = group[:, 6 + k].reshape(B, B)
@@ -386,18 +382,13 @@
                     covar_ref[m, k * B : (k + 1) * B, :] = value
 
     cover(0)
-    relay((4,))
-    for d in (2, 6):
-        from_y(d)
-        over_x(d, 1, 3, 104)
+    relay((1, 7))
+    for d in near[NY]:
+        here = ybuf.at[0, d]
+        remote(here, here, 64, 64 + d, axes["y"][2](other(y, d, NY))).wait_recv()
+        over_z(4, d)
     cover(1)
-    for d in (3, 5):
-        from_y(d)
-        over_x(d, 1, 3, 104)
-    cover(2)
-    from_y(4)
-    over_x(4, 1, 3, 104)
-    cover(3)
+    relay((2, 6))
 
     pts_p = group[:, 4].reshape(B, B)
     left_p, right_p = operand(pts_p, True), operand(pts_p, False)
@@ -412,7 +403,10 @@
     arrived("x", lambda i: diag.at[i], 56)
     w_v[:, 0:B] = kernel_p + diag[...].reshape(B, B)
     w_v[:, B : 2 * B] = jnp.where(eye, 1.0, 0.0)
-    linv = factor_inverse(w_v, dv_v)
+    eliminate(w_v, dv_v, 0, 4)
+    relay((3, 5))
+    eliminate(w_v, dv_v, 4, 8)
+    linv = w_v[:, B : 2 * B] * jnp.sqrt(dv_v[...])
     dv_v[...] = linv
     solved = dot_nt(left6(rowc[...]), right6(linv))
     weights = jnp.dot(left6(solved), right6(linv, 0), preferred_element_type=F32)
@@ -432,26 +426,17 @@
         return carry
 
     lax.fori_loop(0, KC, column, 0, unroll=8)
-
-    for target, send, here in over_x_waits:
-
-        @pl.when(target != c)
-        def _(send=send):
-            send.wait_send()
-
-        @pl.when(target == c)
-        def _(here=here):
-            here.wait()
-
-    for d in near[NC]:
-        peer = other(c, d, NC)
-        for off, first, count in ((96, 0, 1), (104, 1, 3)):
-            here = xbuf.at[peer, first : first + count]
-            remote(here, here, off, off + peer, (r, peer)).wait_recv()
+    cover(2)
+    cover(3)
+
+    for d in (1, 7, 2, 6, 3, 5):
+        from_y(d)
+    for quarter in range(NY):
+        from_z(4, quarter)
     for rel in range(NY):
         for k in range(KR):
             m = k * 4 + other(y, rel, NY)
-            raw = xbuf[:, rel, k].reshape(B, B)
+            raw = jnp.concatenate([ybuf[lax.rem(i + NZ - z, NZ), rel, k] for i in range(NZ)], axis=0)
             rows = pl.ds(pl.multiple_of(m * B, B), B)
             colc_ref[rows, :] = jnp.where(m * NC + c > p, colc_ref[rows, :] + raw, 0.0)
 
@@ -461,6 +446,7 @@
     @pl.when(z != c)
     def _():
         feat_out.wait_send()
+        move.wait_send()
 
 
 def update_kernel(covar_ref, mrow_ref, colc_ref, pf_in, out_ref, pf_ref, out_v, sem):
@@ -522,7 +508,6 @@
             pltpu.VMEM((NY, PART, B), F32),
             pltpu.VMEM((NC, PART, B), F32),
             pltpu.VMEM((NZ, NY, KR, PART, B), F32),
-            pltpu.VMEM((NC, NY, KR, PART, B), F32),
             pltpu.VMEM((KC * B, DEPTH), BF16),
             pltpu.VMEM((KR * B, DEPTH), BF16),
             pltpu.VMEM((KR * B, B), F32),

time: 50.5 us -> 50 us (0.990)
  the two profiles are of different devices: /device:TPU:1 before, /device:TPU:34 now
where the time goes in v4:
time: 50 us; the launch traced here: 49.9 us
  Pallas kernels  48.6 us (97%)
  between operations  1.29 us (3%)
    pallas_call x1, Pallas kernels, body(): pl.pallas_call(gather_kernel, out_shape=(jax.ShapeDtypeStruct((KC, KR * B...  45 us
    pallas_call x1, Pallas kernels, body(): pl.pallas_call(update_kernel, out_shape=(jax.ShapeDtypeStruct((KR * B, KC...  3.63 us

profile of v4, /device:TPU:34, one launch (start us, length us, event | category | flops | bytes accessed | tf_op | source)
XLA Modules:
  0.0 49.9 jit_solution(16557442299669184281)
XLA Ops:
  1.3 45.0 %gather_panel.1 = (f32[16,512,128]{2,1,0:T(8,128)S(1)}, f32[512,128]{1,0:T(8,128)S(1)}, f32[2048,128]{1,0:T(8,128)S(1)}, f32[4,16,128]{2,1,0:T(8,128)S(1)}) custom-call(s32[1]{0:T(128)S(6)} %copy.7.step_ref, f32[4,4,128,128]{3,2,1,0:T(8,128)} %bitcast.6, f32[1,128]{1,0:T(1,128)} %bitcast.7, f32[16,128]{1,0:T(8,128)} %noise_hbm.1, f32[8192,128]{1,0:T(8,128)} %bitcast.5), custom_call_target="tpu_custom_call" | custom-call | tf_op jit(solution)/shard_map/gather_panel/pallas_call | solution.py:482
  46.3 3.6 %update_blocks.1 = (f32[512,16,128]{2,1,0:T(8,128)}, f32[4,16,128]{2,1,0:T(8,128)}) custom-call(f32[16,512,128]{2,1,0:T(8,128)S(1)} %get-tuple-element.8.covar_ref, f32[512,128]{1,0:T(8,128)S(1)} %get-tuple-element.9.mrow_ref, f32[2048,128]{1,0:T(8,128)S(1)} %get-tuple-element.10.colc_ref, f32[4,16,128]{2,1,0:T(8,128)S(1)} %get-tuple-element.11.pf_in), custom_call_target="tpu_custom_call" | custom-call | tf_op jit(solution)/shard_map/update_blocks/pallas_call | solution.py:531

commit v5 on v4

--- a/solution.py
+++ b/solution.py
@@ -73,7 +73,7 @@
     return jnp.concatenate([h, m, h, m, extra], axis=1)
 
 
-def eliminate(w_ref, dv_ref, first, last):
+def eliminate(w_ref, dv_ref):
     size = 16
     lane = lax.broadcasted_iota(jnp.int32, (size, B), 1)
     row = lax.broadcasted_iota(jnp.int32, (size, B), 0)
@@ -108,7 +108,7 @@
         w_ref[...] = w_ref[...] - update
         return carry
 
-    lax.fori_loop(first, last, block, 0)
+    lax.fori_loop(0, B // size, block, 0)
 
 
 def gather_kernel(
@@ -157,8 +157,29 @@
         "z": (z, NZ, lambda i: (y * NZ + i, c)),
         "y": (y, NY, lambda i: (i * NZ + z, c)),
     }
-    partner = (y * NZ + c, z)
     sibling = c + 1 - 2 * lax.rem(c, 2)
+    shifts = ((4, 3), (1, 2), (0, 7), (6, 5))
+
+    def shift_of(chips, core):
+        total = 0
+        for e in range(4):
+            for h in range(2):
+                total = total + jnp.where(jnp.logical_and(chips == e, core == h), shifts[e][h], 0)
+        return total
+
+    def part_at(shift, plane):
+        total = 0
+        for e in range(4):
+            for h in range(2):
+                part = lax.rem(lax.div(plane, 2) + e, 4) * 2 + h
+                total = total + jnp.where(shift == shifts[e][h], part, 0)
+        return total
+
+    chips = lax.rem(lax.div(c, 2) + 4 - lax.div(z, 2), 4)
+    to_row = lax.rem(z + shift_of(chips, lax.rem(c, 2)), NZ)
+    target = (y * NZ + to_row, z)
+    source_part = part_at(lax.rem(z + NZ - c, NZ), c)
+    source = (y * NZ + c, source_part)
     far = {8: (4, 3, 5, 2, 6, 1, 7), 4: (2, 1, 3)}
     near = {8: (1, 7, 2, 6, 3, 5, 4), 4: (1, 3, 2)}
 
@@ -184,9 +205,8 @@
         for d in far[n]:
             pl.semaphore_signal(barrier, inc=1, device_id=dev(other(me, d, n)), device_id_type=MESH)
 
-    @pl.when(z != c)
-    def _():
-        pl.semaphore_signal(barrier, inc=1, device_id=partner, device_id_type=MESH)
+    pl.semaphore_signal(barrier, inc=1, device_id=source, device_id_type=MESH)
+    pl.semaphore_signal(barrier, inc=1, device_id=target, device_id_type=MESH)
 
     def remote(src, dst, send, recv, dev):
         return pltpu.make_async_remote_copy(
@@ -232,13 +252,7 @@
     r_a[c] = s_a[c]
     r_b[c] = s_b[c]
 
-    @pl.when(z != c)
-    def _():
-        pl.semaphore_wait(barrier, 2 * NC + NY - 2)
-
-    @pl.when(z == c)
-    def _():
-        pl.semaphore_wait(barrier, 2 * NC + NY - 3)
+    pl.semaphore_wait(barrier, 2 * NC + NY - 1)
 
     spread("x", lambda i: s_a.at[i], lambda i: r_a.at[i], 0)
     spread("x", lambda i: s_b.at[i], lambda i: r_b.at[i], 8)
@@ -246,18 +260,10 @@
     ls_copy.wait()
     noise_copy.wait()
 
-    part = pl.ds(pl.multiple_of(z * PART, PART), PART)
-    feat_out = remote(feat_v.at[:, y, part, :], group.at[z, 6:10], 24, 24, partner)
-    feat_in = remote(feat_v.at[:, y, part, :], group.at[c, 6:10], 24, 24, partner)
-
-    @pl.when(z != c)
-    def _():
-        feat_out.start()
-
-    @pl.when(z == c)
-    def _():
-        for k in range(KR):
-            group[c, 6 + k] = feat_v[k, y, part, :]
+    part = pl.ds(pl.multiple_of(source_part * PART, PART), PART)
+    feat_out = remote(feat_v.at[:, y, part, :], group.at[source_part, 6:10], 24, 24, source)
+    feat_in = remote(feat_v.at[:, y, part, :], group.at[c, 6:10], 24, 24, source)
+    post(feat_out)
 
     inv_ls = 1.0 / ls_ref[...]
     feat_p = feat_v[lax.div(panel_m, 4), lax.rem(panel_m, 4)] * inv_ls
@@ -280,56 +286,52 @@
 
     arrived("x", lambda i: r_b.at[i], 8)
     group[c, 0:4] = r_b[panel_c]
-    move = remote(group.at[c, 0:4], ybuf.at[0, 0], 25, 25, partner)
-
-    @pl.when(z != c)
-    def _():
-        move.start()
-
-    @pl.when(z == c)
-    def _():
-        ybuf[0, 0] = group[c, 0:4]
+    move = remote(group.at[c, 0:4], ybuf.at[0, 0], 25, 25, target)
+    post(move)
+
+    late = (3, 4, 5)
 
     def over_y(rel):
         for d in near[NY]:
+            if d == 2 and rel not in late:
+                continue
             peer = other(y, d, NY)
             slot = NY - d
-            send = remote(
-                ybuf.at[rel, 0], ybuf.at[rel, slot], 64 + rel * 4 + d, 64 + rel * 4 + slot, axes["y"][2](peer)
+            post(
+                remote(
+                    ybuf.at[rel, 0], ybuf.at[rel, slot], 64 + rel * 4 + d, 64 + rel * 4 + slot, axes["y"][2](peer)
+                )
             )
-            post(send)
-
-    def from_y(rel):
-        for d in near[NY]:
-            peer = other(y, d, NY)
-            here = ybuf.at[rel, d]
-            remote(here, here, 64, 64 + rel * 4 + d, axes["y"][2](peer)).wait_recv()
-
-    def over_z(d, quarter):
-        peer = other(z, d, NZ)
-        sem = 40 if quarter == 0 else 96 + 8 * (quarter - 1)
+
+    def over_y2(rel):
+        side = 3 if rel % 2 == 0 else 1
+        from_y(rel, (side,))
         post(
             remote(
-                ybuf.at[0, quarter], ybuf.at[NZ - d, quarter], sem + d, sem + NZ - d, axes["z"][2](peer)
+                ybuf.at[rel, side],
+                ybuf.at[rel, 2],
+                64 + rel * 4 + 2,
+                64 + rel * 4 + 2,
+                axes["y"][2](other(y, NY - side, NY)),
             )
         )
 
-    def from_z(d, quarter):
-        here = ybuf.at[d, quarter]
-        sem = 40 if quarter == 0 else 96 + 8 * (quarter - 1)
-        remote(here, here, sem, sem + d, axes["z"][2](other(z, d, NZ))).wait_recv()
-
-    def relay(steps):
-        for d in steps:
-            from_z(d, 0)
-            over_y(d)
+    def from_y(rel, sides):
+        for d in sides:
+            here = ybuf.at[rel, d]
+            remote(here, here, 64, 64 + rel * 4 + d, axes["y"][2](other(y, d, NY))).wait_recv()
+
+    def over_z(rel, d, send):
+        slot = (rel - d) % NZ
+        post(remote(ybuf.at[rel, 0], ybuf.at[slot, 0], 40 + send, 40 + slot, axes["z"][2](other(z, d, NZ))))
+
+    def from_z(d):
+        here = ybuf.at[d, 0]
+        remote(here, here, 40, 40 + d, axes["z"][2](other(z, d, NZ))).wait_recv()
 
     arrived("x", lambda i: r_f.at[i], 16)
     group[c, 4:6] = r_f[panel_c]
-
-    @pl.when(z != c)
-    def _():
-        feat_in.wait_recv()
+    feat_in.wait_recv()
 
     mates = [(0, sibling)] + [(d, other(c, d, NC)) for d in (2, 6, 4)]
     for d, peer in mates[1:] + mates[:1]:
@@ -340,6 +342,11 @@
     y_a[y] = z_a[panel_z]
     spread("y", lambda i: y_a.at[y], lambda i: y_a.at[i], 48)
 
+    move.wait_recv()
+    for send, d in enumerate((1, 7, 2, 6)):
+        over_z(0, d, 1 + send)
+    over_y(0)
+
     for d, peer in mates[1:]:
         slot = group.at[peer]
         remote(slot, slot, 120 + d, 120 + peer, (r, peer)).wait_recv()
@@ -349,15 +356,16 @@
     diag[c] = y_a[panel_y]
     spread("x", lambda i: diag.at[c], lambda i: diag.at[i], 56)
 
-    @pl.when(z != c)
-    def _():
-        move.wait_recv()
-
-    for d in near[NZ][:4]:
-        over_z(d, 0)
-    over_y(0)
-    for d in near[NZ][4:]:
-        over_z(d, 0)
+    for d in (1, 7):
+        from_z(d)
+    from_z(6)
+    over_z(6, 1, 5)
+    over_z(6, 2, 6)
+    from_z(2)
+    over_z(2, 7, 7)
+    for rel in (1, 7, 6, 2):
+        over_y(rel)
+    over_y2(0)
 
     for d in (0, 2, 6, 4):
         slot = group.at[other(sibling, d, NC)]
@@ -382,13 +390,15 @@
                     covar_ref[m, k * B : (k + 1) * B, :] = value
 
     cover(0)
-    relay((1, 7))
-    for d in near[NY]:
-        here = ybuf.at[0, d]
-        remote(here, here, 64, 64 + d, axes["y"][2](other(y, d, NY))).wait_recv()
-        over_z(4, d)
+    for rel in (1, 7):
+        over_y2(rel)
+    for rel in (5, 3, 4):
+        from_z(rel)
+        over_y(rel)
     cover(1)
-    relay((2, 6))
+    for rel in (6, 2):
+        over_y2(rel)
+    cover(2)
 
     pts_p = group[:, 4].reshape(B, B)
     left_p, right_p = operand(pts_p, True), operand(pts_p, False)
@@ -398,20 +408,21 @@
     for k in range(KR):
         here = k * NR + r == p
         raw = group[:, k].reshape(B, B)
-        rowc[k * B : (k + 1) * B, :] = kernel_row[k * B : (k + 1) * B, :] + raw + jnp.where(here, noise_p, 0.0)
+        value = kernel_row[k * B : (k + 1) * B, :] + raw + jnp.where(here, noise_p, 0.0)
+        rowc[k * B : (k + 1) * B, :] = left6(value)
 
     arrived("x", lambda i: diag.at[i], 56)
     w_v[:, 0:B] = kernel_p + diag[...].reshape(B, B)
     w_v[:, B : 2 * B] = jnp.where(eye, 1.0, 0.0)
-    eliminate(w_v, dv_v, 0, 4)
-    relay((3, 5))
-    eliminate(w_v, dv_v, 4, 8)
+    eliminate(w_v, dv_v)
     linv = w_v[:, B : 2 * B] * jnp.sqrt(dv_v[...])
     dv_v[...] = linv
-    solved = dot_nt(left6(rowc[...]), right6(linv))
-    weights = jnp.dot(left6(solved), right6(linv, 0), preferred_element_type=F32)
+    inverse = lax.dot_general(
+        left6(linv, 0), right6(linv, 0), (((0,), (0,)), ((), ())), preferred_element_type=F32
+    )
+    weights = dot_nt(rowc[...], right6(inverse))
     share = right6(dv_v[pl.ds(pl.multiple_of(c * PART, PART), PART), :])
-    mine = dot_nt(share, left6(rowc[...]))
+    mine = dot_nt(share, rowc[...])
     row = lax.broadcasted_iota(jnp.int32, (PART, B), 1)
     col = lax.broadcasted_iota(jnp.int32, (PART, B), 0) + c * PART
     for k in range(KR):
@@ -426,27 +437,24 @@
         return carry
 
     lax.fori_loop(0, KC, column, 0, unroll=8)
-    cover(2)
     cover(3)
 
-    for d in (1, 7, 2, 6, 3, 5):
-        from_y(d)
-    for quarter in range(NY):
-        from_z(4, quarter)
+    for rel in (0, 1, 7, 6, 2):
+        from_y(rel, (2, 1) if rel % 2 == 0 else (2, 3))
+    for rel in late:
+        from_y(rel, near[NY])
+    places = [
+        lax.rem(c + shift_of(lax.rem(i // 2 + 4 - lax.div(c, 2), 4), i % 2) + NZ - z, NZ) for i in range(NC)
+    ]
     for rel in range(NY):
         for k in range(KR):
             m = k * 4 + other(y, rel, NY)
-            raw = jnp.concatenate([ybuf[lax.rem(i + NZ - z, NZ), rel, k] for i in range(NZ)], axis=0)
+            raw = jnp.concatenate([ybuf[place, rel, k] for place in places], axis=0)
             rows = pl.ds(pl.multiple_of(m * B, B), B)
             colc_ref[rows, :] = jnp.where(m * NC + c > p, colc_ref[rows, :] + raw, 0.0)
 
     for copy in waits:
         copy.wait_send()
-
-    @pl.when(z != c)
-    def _():
-        feat_out.wait_send()
-        move.wait_send()
 
 
 def update_kernel(covar_ref, mrow_ref, colc_ref, pf_in, out_ref, pf_ref, out_v, sem):
@@ -510,7 +518,7 @@
             pltpu.VMEM((NZ, NY, KR, PART, B), F32),
             pltpu.VMEM((KC * B, DEPTH), BF16),
             pltpu.VMEM((KR * B, DEPTH), BF16),
-            pltpu.VMEM((KR * B, B), F32),
+            pltpu.VMEM((KR * B, 6 * B), BF16),
             pltpu.VMEM((B, 2 * B), F32),
             pltpu.VMEM((B, B), F32),
             pltpu.SemaphoreType.DMA((8,)),

time: 50 us -> 46.7 us (0.934)
  the two profiles are of different devices: /device:TPU:34 before, /device:TPU:32 now
where the time goes in v5:
time: 46.7 us; the launch traced here: 46.6 us
  Pallas kernels  45.3 us (97%)
  between operations  1.29 us (3%)
    pallas_call x1, Pallas kernels, body(): pl.pallas_call(gather_kernel, out_shape=(jax.ShapeDtypeStruct((KC, KR * B...  41.7 us
    pallas_call x1, Pallas kernels, body(): pl.pallas_call(update_kernel, out_shape=(jax.ShapeDtypeStruct((KR * B, KC...  3.63 us

profile of v5, /device:TPU:32, one launch (start us, length us, event | category | flops | bytes accessed | tf_op | source)
XLA Modules:
  0.0 46.6 jit_solution(11995533349504299584)
XLA Ops:
  1.3 41.7 %gather_panel.1 = (f32[16,512,128]{2,1,0:T(8,128)S(1)}, f32[512,128]{1,0:T(8,128)S(1)}, f32[2048,128]{1,0:T(8,128)S(1)}, f32[4,16,128]{2,1,0:T(8,128)S(1)}) custom-call(s32[1]{0:T(128)S(6)} %copy.7.step_ref, f32[4,4,128,128]{3,2,1,0:T(8,128)} %bitcast.6, f32[1,128]{1,0:T(1,128)} %bitcast.7, f32[16,128]{1,0:T(8,128)} %noise_hbm.1, f32[8192,128]{1,0:T(8,128)} %bitcast.5), custom_call_target="tpu_custom_call" | custom-call | tf_op jit(solution)/shard_map/gather_panel/pallas_call | solution.py:490
  43.0 3.6 %update_blocks.1 = (f32[512,16,128]{2,1,0:T(8,128)}, f32[4,16,128]{2,1,0:T(8,128)}) custom-call(f32[16,512,128]{2,1,0:T(8,128)S(1)} %get-tuple-element.8.covar_ref, f32[512,128]{1,0:T(8,128)S(1)} %get-tuple-element.9.mrow_ref, f32[2048,128]{1,0:T(8,128)S(1)} %get-tuple-element.10.colc_ref, f32[4,16,128]{2,1,0:T(8,128)S(1)} %get-tuple-element.11.pf_in), custom_call_target="tpu_custom_call" | custom-call | tf_op jit(solution)/shard_map/update_blocks/pallas_call | solution.py:539

commit v6 on v5

--- a/solution.py
+++ b/solution.py
@@ -73,22 +73,18 @@
     return jnp.concatenate([h, m, h, m, extra], axis=1)
 
 
-def eliminate(w_ref, dv_ref):
+def eliminate(w_ref, dv_ref, between):
     size = 16
     lane = lax.broadcasted_iota(jnp.int32, (size, B), 1)
     row = lax.broadcasted_iota(jnp.int32, (size, B), 0)
-
-    def block(b, carry):
-        start = pl.multiple_of(b * size, size)
-        rows = pl.ds(start, size)
+    for start in range(0, B, size):
+        rows = slice(start, start + size)
         left = w_ref[rows, 0:B]
         right = w_ref[rows, B : 2 * B]
-        rolled = pltpu.roll(left, lax.rem(B - start, B), axis=1)
-        cols = [jnp.broadcast_to(rolled[:, k : k + 1], (size, B)) for k in range(size)]
+        cols = [jnp.broadcast_to(left[:, start + k : start + k + 1], (size, B)) for k in range(size)]
         inv = jnp.zeros((size, B), F32)
         for k in range(size):
-            pivot = jnp.broadcast_to(cols[k][k : k + 1, :], (size, B))
-            rinv = 1.0 / pivot
+            rinv = 1.0 / jnp.broadcast_to(cols[k][k : k + 1, :], (size, B))
             inv = jnp.where(row == k, rinv, inv)
             mult = jnp.where(row > k, cols[k] * rinv, 0.0)
             for j in range(k + 1, size):
@@ -98,17 +94,17 @@
         w_ref[rows, 0:B] = left
         w_ref[rows, B : 2 * B] = right
         dv_ref[rows, :] = inv
-        scaled = jnp.where(lane >= start + size, left * inv, 0.0)
-        update = lax.dot_general(
-            left6(scaled, 0),
-            right6(jnp.concatenate([left, right], axis=1), 0),
-            (((0,), (0,)), ((), ())),
-            preferred_element_type=F32,
-        )
-        w_ref[...] = w_ref[...] - update
-        return carry
-
-    lax.fori_loop(0, B // size, block, 0)
+        end = start + size
+        if end < B:
+            scaled = jnp.where(lane >= end, left * inv, 0.0)
+            update = lax.dot_general(
+                left6(scaled, 0),
+                right6(jnp.concatenate([left, right], axis=1), 0),
+                (((0,), (0,)), ((), ())),
+                preferred_element_type=F32,
+            )
+            w_ref[end:, :] = w_ref[end:, :] - update[end:, :]
+        between(end // size)
 
 
 def gather_kernel(
@@ -289,12 +285,8 @@
     move = remote(group.at[c, 0:4], ybuf.at[0, 0], 25, 25, target)
     post(move)
 
-    late = (3, 4, 5)
-
     def over_y(rel):
         for d in near[NY]:
-            if d == 2 and rel not in late:
-                continue
             peer = other(y, d, NY)
             slot = NY - d
             post(
@@ -303,27 +295,13 @@
                 )
             )
 
-    def over_y2(rel):
-        side = 3 if rel % 2 == 0 else 1
-        from_y(rel, (side,))
-        post(
-            remote(
-                ybuf.at[rel, side],
-                ybuf.at[rel, 2],
-                64 + rel * 4 + 2,
-                64 + rel * 4 + 2,
-                axes["y"][2](other(y, NY - side, NY)),
-            )
-        )
-
-    def from_y(rel, sides):
-        for d in sides:
+    def from_y(rel):
+        for d in near[NY]:
             here = ybuf.at[rel, d]
             remote(here, here, 64, 64 + rel * 4 + d, axes["y"][2](other(y, d, NY))).wait_recv()
 
-    def over_z(rel, d, send):
-        slot = (rel - d) % NZ
-        post(remote(ybuf.at[rel, 0], ybuf.at[slot, 0], 40 + send, 40 + slot, axes["z"][2](other(z, d, NZ))))
+    def over_z(d):
+        post(remote(ybuf.at[0, 0], ybuf.at[NZ - d, 0], 40 + d, 40 + NZ - d, axes["z"][2](other(z, d, NZ))))
 
     def from_z(d):
         here = ybuf.at[d, 0]
@@ -343,9 +321,11 @@
     spread("y", lambda i: y_a.at[y], lambda i: y_a.at[i], 48)
 
     move.wait_recv()
-    for send, d in enumerate((1, 7, 2, 6)):
-        over_z(0, d, 1 + send)
+    for d in near[NZ][:4]:
+        over_z(d)
     over_y(0)
+    for d in near[NZ][4:]:
+        over_z(d)
 
     for d, peer in mates[1:]:
         slot = group.at[peer]
@@ -356,17 +336,12 @@
     diag[c] = y_a[panel_y]
     spread("x", lambda i: diag.at[c], lambda i: diag.at[i], 56)
 
-    for d in (1, 7):
-        from_z(d)
-    from_z(6)
-    over_z(6, 1, 5)
-    over_z(6, 2, 6)
-    from_z(2)
-    over_z(2, 7, 7)
-    for rel in (1, 7, 6, 2):
-        over_y(rel)
-    over_y2(0)
-
+    def relay(*rels):
+        for rel in rels:
+            from_z(rel)
+            over_y(rel)
+
+    relay(1, 7)
     for d in (0, 2, 6, 4):
         slot = group.at[other(sibling, d, NC)]
         remote(slot, slot, 120, 120 + other(sibling, d, NC), (r, sibling)).wait_recv()
@@ -390,15 +365,8 @@
                     covar_ref[m, k * B : (k + 1) * B, :] = value
 
     cover(0)
-    for rel in (1, 7):
-        over_y2(rel)
-    for rel in (5, 3, 4):
-        from_z(rel)
-        over_y(rel)
+    relay(2, 6)
     cover(1)
-    for rel in (6, 2):
-        over_y2(rel)
-    cover(2)
 
     pts_p = group[:, 4].reshape(B, B)
     left_p, right_p = operand(pts_p, True), operand(pts_p, False)
@@ -414,7 +382,14 @@
     arrived("x", lambda i: diag.at[i], 56)
     w_v[:, 0:B] = kernel_p + diag[...].reshape(B, B)
     w_v[:, B : 2 * B] = jnp.where(eye, 1.0, 0.0)
-    eliminate(w_v, dv_v)
+
+    def between(done):
+        if done == 2:
+            relay(3, 5)
+        if done == 4:
+            relay(4)
+
+    eliminate(w_v, dv_v, between)
     linv = w_v[:, B : 2 * B] * jnp.sqrt(dv_v[...])
     dv_v[...] = linv
     inverse = lax.dot_general(
@@ -437,12 +412,11 @@
         return carry
 
     lax.fori_loop(0, KC, column, 0, unroll=8)
+    cover(2)
     cover(3)
 
-    for rel in (0, 1, 7, 6, 2):
-        from_y(rel, (2, 1) if rel % 2 == 0 else (2, 3))
-    for rel in late:
-        from_y(rel, near[NY])
+    for rel in range(NZ):
+        from_y(rel)
     places = [
         lax.rem(c + shift_of(lax.rem(i // 2 + 4 - lax.div(c, 2), 4), i % 2) + NZ - z, NZ) for i in range(NC)
     ]

time: 46.7 us -> 43.8 us (0.938)
  the two profiles are of different devices: /device:TPU:32 before, /device:TPU:7 now
where the time goes in v6:
time: 43.8 us; the launch traced here: 43.7 us
  Pallas kernels  42.4 us (97%)
  between operations  1.29 us (3%)
    pallas_call x1, Pallas kernels, body(): pl.pallas_call(gather_kernel, out_shape=(jax.ShapeDtypeStruct((KC, KR * B...  38.8 us
    pallas_call x1, Pallas kernels, body(): pl.pallas_call(update_kernel, out_shape=(jax.ShapeDtypeStruct((KR * B, KC...  3.63 us

profile of v6, /device:TPU:7, one launch (start us, length us, event | category | flops | bytes accessed | tf_op | source)
XLA Modules:
  0.0 43.7 jit_solution(2284211828806355437)
XLA Ops:
  1.3 38.8 %gather_panel.1 = (f32[16,512,128]{2,1,0:T(8,128)S(1)}, f32[512,128]{1,0:T(8,128)S(1)}, f32[2048,128]{1,0:T(8,128)S(1)}, f32[4,16,128]{2,1,0:T(8,128)S(1)}) custom-call(s32[1]{0:T(128)S(6)} %copy.7.step_ref, f32[4,4,128,128]{3,2,1,0:T(8,128)} %bitcast.6, f32[1,128]{1,0:T(1,128)} %bitcast.7, f32[16,128]{1,0:T(8,128)} %noise_hbm.1, f32[8192,128]{1,0:T(8,128)} %bitcast.5), custom_call_target="tpu_custom_call" | custom-call | tf_op jit(solution)/shard_map/gather_panel/pallas_call | solution.py:464
  40.0 3.6 %update_blocks.1 = (f32[512,16,128]{2,1,0:T(8,128)}, f32[4,16,128]{2,1,0:T(8,128)}) custom-call(f32[16,512,128]{2,1,0:T(8,128)S(1)} %get-tuple-element.8.covar_ref, f32[512,128]{1,0:T(8,128)S(1)} %get-tuple-element.9.mrow_ref, f32[2048,128]{1,0:T(8,128)S(1)} %get-tuple-element.10.colc_ref, f32[4,16,128]{2,1,0:T(8,128)S(1)} %get-tuple-element.11.pf_in), custom_call_target="tpu_custom_call" | custom-call | tf_op jit(solution)/shard_map/update_blocks/pallas_call | solution.py:513

commit v7 on v6

--- a/solution.py
+++ b/solution.py
@@ -303,6 +303,9 @@
     def over_z(d):
         post(remote(ybuf.at[0, 0], ybuf.at[NZ - d, 0], 40 + d, 40 + NZ - d, axes["z"][2](other(z, d, NZ))))
 
+    def over_z4(slot):
+        post(remote(ybuf.at[0, slot], ybuf.at[4, slot], 96 + slot, 96 + slot, axes["z"][2](other(z, 4, NZ))))
+
     def from_z(d):
         here = ybuf.at[d, 0]
         remote(here, here, 40, 40 + d, axes["z"][2](other(z, d, NZ))).wait_recv()
@@ -365,8 +368,12 @@
                     covar_ref[m, k * B : (k + 1) * B, :] = value
 
     cover(0)
+    from_y(0)
+    for slot in range(1, NY):
+        over_z4(slot)
     relay(2, 6)
     cover(1)
+    cover(2)
 
     pts_p = group[:, 4].reshape(B, B)
     left_p, right_p = operand(pts_p, True), operand(pts_p, False)
@@ -386,8 +393,6 @@
     def between(done):
         if done == 2:
             relay(3, 5)
-        if done == 4:
-            relay(4)
 
     eliminate(w_v, dv_v, between)
     linv = w_v[:, B : 2 * B] * jnp.sqrt(dv_v[...])
@@ -412,11 +417,14 @@
         return carry
 
     lax.fori_loop(0, KC, column, 0, unroll=8)
-    cover(2)
     cover(3)
 
-    for rel in range(NZ):
+    for rel in (1, 7, 2, 6, 3, 5):
         from_y(rel)
+    from_z(4)
+    for slot in range(1, NY):
+        far_z = ybuf.at[4, slot]
+        remote(far_z, far_z, 96, 96 + slot, axes["z"][2](other(z, 4, NZ))).wait_recv()
     places = [
         lax.rem(c + shift_of(lax.rem(i // 2 + 4 - lax.div(c, 2), 4), i % 2) + NZ - z, NZ) for i in range(NC)
     ]

time: 43.8 us -> 42.8 us (0.977)
  the two profiles are of different devices: /device:TPU:7 before, /device:TPU:16 now
where the time goes in v7:
time: 42.8 us
  Pallas kernels  41.5 us (97%)
  between operations  1.29 us (3%)
    pallas_call x1, Pallas kernels, body(): pl.pallas_call(gather_kernel, out_shape=(jax.ShapeDtypeStruct((KC, KR * B...  37.8 us
    pallas_call x1, Pallas kernels, body(): pl.pallas_call(update_kernel, out_shape=(jax.ShapeDtypeStruct((KR * B, KC...  3.64 us

profile of v7, /device:TPU:16, one launch (start us, length us, event | category | flops | bytes accessed | tf_op | source)
XLA Modules:
  0.0 42.8 jit_solution(16805029244828021395)
XLA Ops:
  1.3 37.8 %gather_panel.1 = (f32[16,512,128]{2,1,0:T(8,128)S(1)}, f32[512,128]{1,0:T(8,128)S(1)}, f32[2048,128]{1,0:T(8,128)S(1)}, f32[4,16,128]{2,1,0:T(8,128)S(1)}) custom-call(s32[1]{0:T(128)S(6)} %copy.7.step_ref, f32[4,4,128,128]{3,2,1,0:T(8,128)} %bitcast.6, f32[1,128]{1,0:T(1,128)} %bitcast.7, f32[16,128]{1,0:T(8,128)} %noise_hbm.1, f32[8192,128]{1,0:T(8,128)} %bitcast.5), custom_call_target="tpu_custom_call" | custom-call | tf_op jit(solution)/shard_map/gather_panel/pallas_call | solution.py:472
  39.1 3.6 %update_blocks.1 = (f32[512,16,128]{2,1,0:T(8,128)}, f32[4,16,128]{2,1,0:T(8,128)}) custom-call(f32[16,512,128]{2,1,0:T(8,128)S(1)} %get-tuple-element.8.covar_ref, f32[512,128]{1,0:T(8,128)S(1)} %get-tuple-element.9.mrow_ref, f32[2048,128]{1,0:T(8,128)S(1)} %get-tuple-element.10.colc_ref, f32[4,16,128]{2,1,0:T(8,128)S(1)} %get-tuple-element.11.pf_in), custom_call_target="tpu_custom_call" | custom-call | tf_op jit(solution)/shard_map/update_blocks/pallas_call | solution.py:521

commit v8 on v7

--- a/solution.py
+++ b/solution.py
@@ -73,7 +73,7 @@
     return jnp.concatenate([h, m, h, m, extra], axis=1)
 
 
-def eliminate(w_ref, dv_ref, between):
+def eliminate(w_ref, dv_ref):
     size = 16
     lane = lax.broadcasted_iota(jnp.int32, (size, B), 1)
     row = lax.broadcasted_iota(jnp.int32, (size, B), 0)
@@ -104,7 +104,6 @@
                 preferred_element_type=F32,
             )
             w_ref[end:, :] = w_ref[end:, :] - update[end:, :]
-        between(end // size)
 
 
 def gather_kernel(
@@ -176,6 +175,10 @@
     target = (y * NZ + to_row, z)
     source_part = part_at(lax.rem(z + NZ - c, NZ), c)
     source = (y * NZ + c, source_part)
+    far_rows = (3, 5)
+    far_parts = {rel: part_at(lax.rem(z + rel + NZ - c, NZ), c) for rel in far_rows}
+    far_local = {rel: jnp.logical_and(z == c, far_parts[rel] == c) for rel in far_rows}
+    far_targets = {rel: lax.rem(to_row + NZ - rel, NZ) for rel in far_rows}
     far = {8: (4, 3, 5, 2, 6, 1, 7), 4: (2, 1, 3)}
     near = {8: (1, 7, 2, 6, 3, 5, 4), 4: (1, 3, 2)}
 
@@ -203,6 +206,13 @@
 
     pl.semaphore_signal(barrier, inc=1, device_id=source, device_id_type=MESH)
     pl.semaphore_signal(barrier, inc=1, device_id=target, device_id_type=MESH)
+    for rel in far_rows:
+
+        @pl.when(jnp.logical_not(far_local[rel]))
+        def _(rel=rel):
+            pl.semaphore_signal(
+                barrier, inc=1, device_id=(y * NZ + c, far_parts[rel]), device_id_type=MESH
+            )
 
     def remote(src, dst, send, recv, dev):
         return pltpu.make_async_remote_copy(
@@ -248,7 +258,15 @@
     r_a[c] = s_a[c]
     r_b[c] = s_b[c]
 
-    pl.semaphore_wait(barrier, 2 * NC + NY - 1)
+    alone = jnp.logical_and(z == c, lax.rem(c, 2) == 1)
+
+    @pl.when(jnp.logical_not(alone))
+    def _():
+        pl.semaphore_wait(barrier, 2 * NC + NY + 1)
+
+    @pl.when(alone)
+    def _():
+        pl.semaphore_wait(barrier, 2 * NC + NY)
 
     spread("x", lambda i: s_a.at[i], lambda i: r_a.at[i], 0)
     spread("x", lambda i: s_b.at[i], lambda i: r_b.at[i], 8)
@@ -284,6 +302,21 @@
     group[c, 0:4] = r_b[panel_c]
     move = remote(group.at[c, 0:4], ybuf.at[0, 0], 25, 25, target)
     post(move)
+    far_moves = []
+    for rel in far_rows:
+        far_move = remote(
+            group.at[c, 0:4], ybuf.at[rel, 0], 40 + rel, 40 + rel, (y * NZ + far_targets[rel], z)
+        )
+        stays = jnp.logical_and(z == c, far_targets[rel] == z)
+        far_moves.append((far_move, stays))
+
+        @pl.when(jnp.logical_not(stays))
+        def _(far_move=far_move):
+            far_move.start()
+
+        @pl.when(stays)
+        def _(rel=rel):
+            ybuf[rel, 0] = group[c, 0:4]
 
     def over_y(rel):
         for d in near[NY]:
@@ -308,7 +341,14 @@
 
     def from_z(d):
         here = ybuf.at[d, 0]
-        remote(here, here, 40, 40 + d, axes["z"][2](other(z, d, NZ))).wait_recv()
+        landed = remote(here, here, 40, 40 + d, axes["z"][2](other(z, d, NZ)))
+        if d not in far_rows:
+            landed.wait_recv()
+            return
+
+        @pl.when(jnp.logical_not(far_local[d]))
+        def _():
+            landed.wait_recv()
 
     arrived("x", lambda i: r_f.at[i], 16)
     group[c, 4:6] = r_f[panel_c]
@@ -324,11 +364,9 @@
     spread("y", lambda i: y_a.at[y], lambda i: y_a.at[i], 48)
 
     move.wait_recv()
-    for d in near[NZ][:4]:
+    for d in (1, 7, 2, 6, 4):
         over_z(d)
     over_y(0)
-    for d in near[NZ][4:]:
-        over_z(d)
 
     for d, peer in mates[1:]:
         slot = group.at[peer]
@@ -371,6 +409,7 @@
     from_y(0)
     for slot in range(1, NY):
         over_z4(slot)
+    relay(3, 5)
     relay(2, 6)
     cover(1)
     cover(2)
@@ -390,11 +429,7 @@
     w_v[:, 0:B] = kernel_p + diag[...].reshape(B, B)
     w_v[:, B : 2 * B] = jnp.where(eye, 1.0, 0.0)
 
-    def between(done):
-        if done == 2:
-            relay(3, 5)
-
-    eliminate(w_v, dv_v, between)
+    eliminate(w_v, dv_v)
     linv = w_v[:, B : 2 * B] * jnp.sqrt(dv_v[...])
     dv_v[...] = linv
     inverse = lax.dot_general(
@@ -411,12 +446,9 @@
         keep = jnp.logical_or(w > p, jnp.logical_and(w == p, col <= row))
         pf_ref[k] = jnp.where(keep, mine[:, k * B : (k + 1) * B], 0.0)
 
-    def column(m, carry):
-        rows = pl.ds(pl.multiple_of(m * B, B), B)
+    for quarter in range(4):
+        rows = slice(quarter * 4 * B, (quarter + 1) * 4 * B)
         colc_ref[rows, :] = jnp.exp(dot_nt(colcat[rows, :], left_p))
-        return carry
-
-    lax.fori_loop(0, KC, column, 0, unroll=8)
     cover(3)
 
     for rel in (1, 7, 2, 6, 3, 5):
@@ -437,6 +469,11 @@
 
     for copy in waits:
         copy.wait_send()
+    for far_move, stays in far_moves:
+
+        @pl.when(jnp.logical_not(stays))
+        def _(far_move=far_move):
+            far_move.wait_send()
 
 
 def update_kernel(covar_ref, mrow_ref, colc_ref, pf_in, out_ref, pf_ref, out_v, sem):

time: 42.8 us -> 43.4 us (1.014)
  the two profiles are of different devices: /device:TPU:16 before, /device:TPU:1 now
where the time goes in v8:
time: 43.4 us; the launch traced here: 43.3 us
  Pallas kernels  42 us (97%)
  between operations  1.29 us (3%)
    pallas_call x1, Pallas kernels, body(): pl.pallas_call(gather_kernel, out_shape=(jax.ShapeDtypeStruct((KC, KR * B...  38.4 us
    pallas_call x1, Pallas kernels, body(): pl.pallas_call(update_kernel, out_shape=(jax.ShapeDtypeStruct((KR * B, KC...  3.63 us

profile of v8, /device:TPU:1, one launch (start us, length us, event | category | flops | bytes accessed | tf_op | source)
XLA Modules:
  0.0 43.3 jit_solution(953610814218356285)
XLA Ops:
  1.3 38.4 %gather_panel.1 = (f32[16,512,128]{2,1,0:T(8,128)S(1)}, f32[512,128]{1,0:T(8,128)S(1)}, f32[2048,128]{1,0:T(8,128)S(1)}, f32[4,16,128]{2,1,0:T(8,128)S(1)}) custom-call(s32[1]{0:T(128)S(6)} %copy.7.step_ref, f32[4,4,128,128]{3,2,1,0:T(8,128)} %bitcast.6, f32[1,128]{1,0:T(1,128)} %bitcast.7, f32[16,128]{1,0:T(8,128)} %noise_hbm.1, f32[8192,128]{1,0:T(8,128)} %bitcast.5), custom_call_target="tpu_custom_call" | custom-call | tf_op jit(solution)/shard_map/gather_panel/pallas_call | solution.py:509
  39.7 3.6 %update_blocks.1 = (f32[512,16,128]{2,1,0:T(8,128)}, f32[4,16,128]{2,1,0:T(8,128)}) custom-call(f32[16,512,128]{2,1,0:T(8,128)S(1)} %get-tuple-element.8.covar_ref, f32[512,128]{1,0:T(8,128)S(1)} %get-tuple-element.9.mrow_ref, f32[2048,128]{1,0:T(8,128)S(1)} %get-tuple-element.10.colc_ref, f32[4,16,128]{2,1,0:T(8,128)S(1)} %get-tuple-element.11.pf_in), custom_call_target="tpu_custom_call" | custom-call | tf_op jit(solution)/shard_map/update_blocks/pallas_call | solution.py:558

commit v9 on v7

--- a/solution.py
+++ b/solution.py
@@ -411,12 +411,9 @@
         keep = jnp.logical_or(w > p, jnp.logical_and(w == p, col <= row))
         pf_ref[k] = jnp.where(keep, mine[:, k * B : (k + 1) * B], 0.0)
 
-    def column(m, carry):
-        rows = pl.ds(pl.multiple_of(m * B, B), B)
+    for quarter in range(4):
+        rows = slice(quarter * 4 * B, (quarter + 1) * 4 * B)
         colc_ref[rows, :] = jnp.exp(dot_nt(colcat[rows, :], left_p))
-        return carry
-
-    lax.fori_loop(0, KC, column, 0, unroll=8)
     cover(3)
 
     for rel in (1, 7, 2, 6, 3, 5):

time: 42.8 us -> 42.6 us (level)
  the two profiles are of different devices: /device:TPU:16 before, /device:TPU:8 now
where the time goes in v9:
time: 42.6 us; the launch traced here: 42.5 us
  Pallas kernels  41.2 us (97%)
  between operations  1.29 us (3%)
    pallas_call x1, Pallas kernels, body(): pl.pallas_call(gather_kernel, out_shape=(jax.ShapeDtypeStruct((KC, KR * B...  37.6 us
    pallas_call x1, Pallas kernels, body(): pl.pallas_call(update_kernel, out_shape=(jax.ShapeDtypeStruct((KR * B, KC...  3.63 us

profile of v9, /device:TPU:8, one launch (start us, length us, event | category | flops | bytes accessed | tf_op | source)
XLA Modules:
  0.0 42.5 jit_solution(13267673288509442905)
XLA Ops:
  1.3 37.6 %gather_panel.1 = (f32[16,512,128]{2,1,0:T(8,128)S(1)}, f32[512,128]{1,0:T(8,128)S(1)}, f32[2048,128]{1,0:T(8,128)S(1)}, f32[4,16,128]{2,1,0:T(8,128)S(1)}) custom-call(s32[1]{0:T(128)S(6)} %copy.7.step_ref, f32[4,4,128,128]{3,2,1,0:T(8,128)} %bitcast.6, f32[1,128]{1,0:T(1,128)} %bitcast.7, f32[16,128]{1,0:T(8,128)} %noise_hbm.1, f32[8192,128]{1,0:T(8,128)} %bitcast.5), custom_call_target="tpu_custom_call" | custom-call | tf_op jit(solution)/shard_map/gather_panel/pallas_call | solution.py:469
  38.8 3.6 %update_blocks.1 = (f32[512,16,128]{2,1,0:T(8,128)}, f32[4,16,128]{2,1,0:T(8,128)}) custom-call(f32[16,512,128]{2,1,0:T(8,128)S(1)} %get-tuple-element.8.covar_ref, f32[512,128]{1,0:T(8,128)S(1)} %get-tuple-element.9.mrow_ref, f32[2048,128]{1,0:T(8,128)S(1)} %get-tuple-element.10.colc_ref, f32[4,16,128]{2,1,0:T(8,128)S(1)} %get-tuple-element.11.pf_in), custom_call_target="tpu_custom_call" | custom-call | tf_op jit(solution)/shard_map/update_blocks/pallas_call | solution.py:518
